TPU v7x, 32 devices: a whole 2x2x4 slice. The times are simulated.
32 devices in a mesh: gx: 4 (over y, x), gy: 8 (over z, core).
Axes of the slice: x: 2, y: 2, z: 4, core: 2. Of those that a mesh axis runs over, the one named last changes fastest.
Arguments:
- terminal_elevation: float32 [8, 1024, 1024], P(None, 'gx', 'gy'), may hold values from -6 to 6
- terminal_flux_x: float32 [8, 1024, 1024], P(None, 'gx', 'gy'), may hold values from -6 to 6
- terminal_flux_y: float32 [8, 1024, 1024], P(None, 'gx', 'gy'), may hold values from -6 to 6
- courant_x: float32 [1024, 1024], P('gx', 'gy'), may hold values from 0 to 0.45, as said below
- courant_y: float32 [1024, 1024], P('gx', 'gy'), may hold values from 0 to 0.45, as said below
- land_sea: int32 [1024, 1024], P('gx', 'gy'), may hold values from 0 to 1
- uplift: float32 [1024, 1024], P('gx', 'gy'), may hold values from 0.1 to 1
- tile_patches: int32 [4, 8, 15], replicated, may hold values from 0 to 255, as said below
- patch_home: int32 [256], replicated, may hold values from 0 to 255, each once
Outputs:
- adjoint_elevation: float32 [8, 1024, 1024], P(None, 'gx', 'gy')
- patch_gradient: float32 [256, 8], P(('gx', 'gy'))
Inputs may be any that keep to these rules, and one draw needn't show every extreme that they name: tile_patches[a, b, s] for s = u * 3 + w is the patch whose footprint covers the cells of tile a, b at slot s; footprints are squares of 64 cells offset by 32, the last one wrapping to the first, so every patch is listed by one to four tiles consistently. `courant_x`: zero on every face next to a land cell and on the faces past the grid's last row; sums of the two numbers of a cell stay under one. `courant_y`: zero on every face next to a land cell and on the faces past the grid's last column.
All inputs are finite; a program needn't handle non-finite values.
Results may differ from a plain program's by a relative error of at most 0.00026.
Values sent between devices are 32-bit elements; how exact they have to be, the bound alone decides.
No kernel may reach another device: no remote copies, remote signals or barrier semaphores. Data moves between devices by JAX's collectives and lax.ppermute only.
A program may use at most 64 MiB of HBM per device.

v0:
```python
import jax
import jax.numpy as jnp
from jax import lax
from jax.experimental import pallas as pl
from jax.experimental.pallas import tpu as pltpu
from jax.sharding import PartitionSpec as P

BS = 64
ITERS = 8
LANES = 128
W = 8
GROUPS = LANES // W
F32 = jnp.float32
VMEM = pl.BlockSpec(memory_space=pltpu.VMEM)
SMEM = pl.BlockSpec(memory_space=pltpu.SMEM)
HBM = pl.BlockSpec(memory_space=pl.ANY)


def lanes_of(shape=(8, LANES)):
    return lax.broadcasted_iota(jnp.int32, shape, len(shape) - 1)


def roll(vector, distance):
    distance = distance % LANES
    return pltpu.roll(vector, distance, vector.ndim - 1) if distance else vector


def params(mebibytes):
    return pltpu.CompilerParams(vmem_limit_bytes=mebibytes * 2**20)


def tile(ref, row):
    return ref[pl.ds(row if isinstance(row, int) else pl.multiple_of(row, 8), 8), :]


def payload_layout(rows):
    heights = rows // GROUPS
    tiles = rows // 8 // GROUPS
    return (0, heights, 2 * heights, 2 * heights + tiles, 2 * heights + 2 * tiles)


def load_kernel(rows, h_hbm, x_hbm, y_hbm, cx_ref, cy_ref, wet_ref, h_out, d_out, even_out, odd_out, hb, xb, yb, sems):
    gauges = 8
    parts = 4
    size = rows // parts

    def piece(part, source, target, gauge):
        return pltpu.make_async_copy(
            source.at[pl.ds(gauge * rows + part * size, size)],
            target.at[pl.ds(part * size, size), gauge],
            sems.at[part],
        )

    for part in range(parts):
        for source, target in ((h_hbm, hb), (x_hbm, xb), (y_hbm, yb)):
            for gauge in range(gauges):
                piece(part, source, target, gauge).start()

    even = lax.rem(lax.axis_index("gy"), 2) == 0
    lane = lanes_of()
    group = lane // W
    at_h, at_d, at_cx, at_cy, at_g = payload_layout(rows)

    def put(place, to_left, to_right):
        even_out[place] = jnp.where(even, to_right, to_left)
        odd_out[place] = jnp.where(even, to_left, to_right)

    for ref, place in ((cx_ref, at_cx), (cy_ref, at_cy)):
        for p in range(rows // 8 // GROUPS):
            to_left = to_right = jnp.zeros((8, LANES), F32)
            for k in range(GROUPS):
                value = ref[pl.ds((p * GROUPS + k) * 8, 8), :]
                to_left = jnp.where(group == k, roll(value, W * k), to_left)
                to_right = jnp.where(group == k, roll(value, W * k + W), to_right)
            put(place + p, to_left, to_right)

    def block(m, above):
        lefts = [jnp.zeros((8, LANES), F32)] * 2
        rights = [jnp.zeros((8, LANES), F32)] * 2
        for k in range(GROUPS):
            r = m * GROUPS + k
            cx = cx_ref[pl.ds(r, 1), :]
            cy = cy_ref[pl.ds(r, 1), :]
            wet = wet_ref[pl.ds(r, 1), :].astype(F32)
            along_x = cx * xb[r]
            along_y = cy * yb[r]
            before_y = roll(along_y, 1)
            height = wet * hb[r]
            part = (along_x - above) + along_y
            divergence = part - jnp.where(lane == 0, 0.0, before_y)
            outgoing = jnp.where(lane == 0, -before_y, divergence)
            above = along_x
            h_out[r] = height
            d_out[r] = divergence
            mine = group == k
            lefts = [
                jnp.where(mine, roll(height, W * k), lefts[0]),
                jnp.where(mine, roll(divergence, W * k), lefts[1]),
            ]
            rights = [
                jnp.where(mine, roll(height, W * k + W), rights[0]),
                jnp.where(mine, roll(outgoing, W * k + W - 1), rights[1]),
            ]
        put(at_h + m, lefts[0], rights[0])
        put(at_d + m, lefts[1], rights[1])
        return above

    above = jnp.zeros((8, LANES), F32)
    blocks = size // GROUPS
    for part in range(parts):
        done = hb.at[pl.ds(0, 3 * size)] if 3 * size <= rows else None
        pltpu.make_async_copy(done, done, sems.at[part]).wait()
        above = lax.fori_loop(part * blocks, (part + 1) * blocks, block, above)
    h_out[rows] = jnp.zeros((8, LANES), F32)
    d_out[rows] = -above
    put(at_g, -above, roll(-above, W))


def row_step(h_in, d_in, h_out, d_out, cx_ref, cy_ref, r, height, before):
    following = h_in[r + 1]
    along_x = cx_ref[pl.ds(r, 1), :] * (following - height)
    along_y = cy_ref[pl.ds(r, 1), :] * (roll(height, LANES - 1) - height)
    divergence = d_in[r] + ((along_x - before) + (along_y - roll(along_y, 1)))
    d_out[r] = divergence
    h_out[r] = height + divergence
    return following, along_x


def sweep(rows, unroll, h_in, d_in, h_out, d_out, cx_ref, cy_ref):
    def block(b, carry):
        height, before = carry
        for k in range(unroll):
            height, before = row_step(
                h_in, d_in, h_out, d_out, cx_ref, cy_ref, b * unroll + k, height, before
            )
        return height, before

    lax.fori_loop(0, rows // unroll, block, (h_in[0], jnp.zeros((8, LANES), F32)))


def run_steps(rows, h_in, d_in, h_out, d_out, cx_ref, cy_ref):
    h_out[rows] = jnp.zeros((8, LANES), F32)
    sweep(rows, 16, h_in, d_in, h_out, d_out, cx_ref, cy_ref)

    def again(t, carry):
        sweep(rows, 16, h_out, d_out, h_out, d_out, cx_ref, cy_ref)
        return carry

    lax.fori_loop(1, ITERS, again, 0)


def center_kernel(rows, h_ref, d_ref, cx_ref, cy_ref, h_out, d_work):
    run_steps(rows, h_ref, d_ref, h_out, d_work, cx_ref, cy_ref)


def strip(lane, own, from_left, from_right):
    return jnp.where(
        lane >= LANES - 2 * W,
        own,
        jnp.where(lane < W, from_right, jnp.where(lane < 64, from_left, roll(own, 64))),
    )


def strip_divergence(lane, own, from_left, from_right):
    middle = jnp.where(lane >= 64, roll(own, 64), 0.0) + jnp.where(
        (lane > 64 - W) & (lane <= 64), from_left, 0.0
    )
    return jnp.where(lane >= LANES - 2 * W, own, jnp.where(lane < W, from_right, middle))


class Sides:
    def __init__(self, even_in, odd_in, even_out, odd_out):
        self.even = lax.rem(lax.axis_index("gy"), 2) == 0
        self.lane = lanes_of()
        self.refs = (even_in, odd_in, even_out, odd_out)

    def left(self, place):
        even_in, odd_in, _, _ = self.refs
        return jnp.where(self.even, odd_in[place], even_in[place])

    def right(self, place):
        even_in, odd_in, _, _ = self.refs
        return jnp.where(self.even, even_in[place], odd_in[place])

    def right_divergence(self, place):
        _, _, even_out, odd_out = self.refs
        sent = jnp.where(self.even, even_out[place], odd_out[place])
        return self.right(place) + jnp.where(self.lane % W == 0, roll(sent, -(W - 1)), 0.0)


def middle_kernel(rows, even_in, odd_in, even_out, odd_out, h_ref, d_ref, cx_ref, cy_ref, x_even, x_odd):
    side = Sides(even_in, odd_in, even_out, odd_out)
    lane, group = side.lane, side.lane // W
    at_h, at_d, at_cx, at_cy, at_g = payload_layout(rows)
    last_h, last_c = rows // GROUPS - 1, rows // 8 // GROUPS - 1
    even = lax.rem(lax.axis_index("gx"), 2) == 0

    def put(place, up, down):
        x_even[place] = jnp.where(even, down, up)
        x_odd[place] = jnp.where(even, up, down)

    for j in range(W):
        put(j, h_ref[j], h_ref[rows - W + j])
        put(W + j, d_ref[j], d_ref[rows - W + j])
    first = lane < 64
    put(
        2 * W,
        jnp.where(first, side.left(at_h), roll(side.right(at_h), 64)),
        jnp.where(first, roll(side.left(at_h + last_h), 64), side.right(at_h + last_h)),
    )
    put(
        2 * W + 1,
        jnp.where(first, side.left(at_d), roll(side.right_divergence(at_d), 64)),
        jnp.where(first, roll(side.left(at_d + last_h), 64), side.right_divergence(at_d + last_h)),
    )
    put(2 * W + 2, cx_ref[0:8, :], cx_ref[rows - 8 : rows, :])
    put(2 * W + 3, cy_ref[0:8, :], cy_ref[rows - 8 : rows, :])

    def gathered(pieces):
        result = pieces[0]
        for k, piece in enumerate(pieces[1:], 1):
            result = jnp.where(group == k, roll(piece, W * k), result)
        return result

    g_left, g_right = side.left(at_g), side.right(at_g)
    put(
        2 * W + 4,
        gathered([side.left(at_cx), side.right(at_cx), side.left(at_cy), side.right(at_cy), g_left, g_right]),
        gathered(
            [roll(side.left(at_cx + last_c), W), roll(side.right(at_cx + last_c), W)]
            + [roll(side.left(at_cy + last_c), W), roll(side.right(at_cy + last_c), W)]
            + [g_left, g_right]
        ),
    )
    put(2 * W + 5, d_ref[rows], d_ref[rows])


MESSAGE = 2 * W + 6


def strips_kernel(
    rows, even_in, odd_in, even_out, odd_out, h_ref, d_ref, cx_ref, cy_ref, done_ref, wet_ref, uplift_ref, lists_ref, home_ref,
    out_hbm, bh0, bd0, cbx, cby, hb, sums, homes, db, merged, sem,
):
    side = Sides(even_in, odd_in, even_out, odd_out)
    lane = side.lane
    at_h, at_d, at_cx, at_cy, at_g = payload_layout(rows)
    for ref, target, place in ((cx_ref, cbx, at_cx), (cy_ref, cby, at_cy)):
        for p in range(rows // 8 // GROUPS):
            left, right = side.left(place + p), side.right(place + p)
            for k in range(GROUPS):
                q = (p * GROUPS + k) * 8
                target[pl.ds(q, 8), :] = strip(
                    lane, ref[pl.ds(q, 8), :], roll(left, 64 - W - W * k), roll(right, -W * k)
                )

    def build(m, carry):
        h_left, h_right = side.left(at_h + m), side.right(at_h + m)
        d_left, d_right = side.left(at_d + m), side.right_divergence(at_d + m)
        for k in range(GROUPS):
            r = m * GROUPS + k
            bh0[r] = strip(lane, h_ref[r], roll(h_left, 64 - W - W * k), roll(h_right, -W * k))
            bd0[r] = strip_divergence(
                lane, d_ref[r], roll(d_left, 64 - W + 1 - W * k), roll(d_right, -W * k)
            )
        return carry

    lax.fori_loop(0, rows // GROUPS, build, 0)
    bh0[rows] = jnp.zeros((8, LANES), F32)
    bd0[rows] = strip(lane, d_ref[rows], roll(side.left(at_g), 64 - W), side.right(at_g))
    run_steps(rows, bh0, bd0, hb, db, cbx, cby)

    def weigh(b, total):
        for k in range(8):
            r = b * 8 + k
            value = merge(lane, done_ref[r], hb[r])
            merged[r] = value
            weight = wet_ref[pl.ds(r, 1), :].astype(F32) * uplift_ref[pl.ds(r, 1), :] * (1.0 / BS)
            total = total + weight * value
        return total

    bounds = slot_bounds(rows)
    for u in range(len(bounds) - 1):
        low, high = max(bounds[u], W) // 8, min(bounds[u + 1], rows - W) // 8
        sums[u] = lax.fori_loop(low, high, weigh, jnp.zeros((8, LANES), F32))
    count = rows - 2 * W
    copies = [
        pltpu.make_async_copy(merged.at[pl.ds(W, count), g], out_hbm.at[pl.ds(g * rows + W, count)], sem)
        for g in range(8)
    ]
    for copy in copies:
        copy.start()

    tile_at = lax.axis_index("gx") * lax.axis_size("gy") + lax.axis_index("gy")
    slots = homes.shape[0]
    for s in range(slots):
        patch = lists_ref[tile_at * slots + s]
        homes[pl.ds(s, 1), :] = jnp.full((1, LANES), home_ref[patch], jnp.int32)
    for copy in copies:
        copy.wait()


def merge(lane, center, strips):
    return jnp.where(lane < W, roll(strips, 64), jnp.where(lane >= LANES - W, strips, center))


def slot_bounds(length):
    return [0] + list(range(BS // 2, length, BS)) + [length]


def bands_kernel(
    rows, x_even_in, x_odd_in, h_ref, d_ref, cx_ref, cy_ref, bh0, bd0, cbx, cby, done_wet, uplift_ref, sums_ref, homes_ref, out_in,
    out_hbm, message, hs, ds, cxs, cys, edge, sem,
):
    lane = lanes_of()
    even = lax.rem(lax.axis_index("gx"), 2) == 0
    depth = 3 * W

    def above(place):
        return jnp.where(even, x_odd_in[place], x_even_in[place])

    def below(place):
        return jnp.where(even, x_even_in[place], x_odd_in[place])

    for band, (got, halo_at, own_at, own_row) in enumerate(
        ((above, 0, W, 0), (below, 2 * W, 0, rows - 2 * W))
    ):
        center, side = 2 * band, 2 * band + 1
        packed_h, packed_d, packed_c = got(2 * W), got(2 * W + 1), got(2 * W + 4)
        for j in range(W):
            height, divergence = got(j), got(W + j)
            hs[center, halo_at + j] = height
            ds[center, halo_at + j] = divergence
            hs[side, halo_at + j] = strip(
                lane, height, roll(packed_h, 64 - W - W * j), roll(packed_h, -64 - W * j)
            )
            ds[side, halo_at + j] = strip_divergence(
                lane, divergence, roll(packed_d, 64 - W + 1 - W * j), roll(packed_d, -64 - W * j)
            )
        for c, (ref, mine, strips) in enumerate(((cxs, cx_ref, cbx), (cys, cy_ref, cby))):
            value = got(2 * W + 2 + c)
            ref[center, pl.ds(halo_at, W), :] = value
            ref[side, pl.ds(halo_at, W), :] = strip(
                lane, value, roll(packed_c, 64 - W - 2 * W * c), roll(packed_c, -W - 2 * W * c)
            )
            ref[center, pl.ds(own_at, 2 * W), :] = mine[pl.ds(own_row, 2 * W), :]
            ref[side, pl.ds(own_at, 2 * W), :] = strips[pl.ds(own_row, 2 * W), :]
        for j in range(2 * W):
            hs[center, own_at + j] = h_ref[own_row + j]
            ds[center, own_at + j] = d_ref[own_row + j]
            hs[side, own_at + j] = bh0[own_row + j]
            ds[side, own_at + j] = bd0[own_row + j]
        if band == 0:
            flux = got(2 * W + 5)
            ds[center, W] = ds[center, W] + flux
            ds[side, W] = ds[side, W] + strip(
                lane, flux, roll(packed_c, 64 - W - 4 * W), roll(packed_c, -5 * W)
            )
        else:
            ds[center, 2 * W] = ds[center, 2 * W] + d_ref[rows]
            ds[side, 2 * W] = ds[side, 2 * W] + bd0[rows]
        for b in (center, side):
            hs[b, depth] = jnp.zeros((8, LANES), F32)

    def step(t, carry):
        state = [(hs[b, 0], jnp.zeros((8, LANES), F32)) for b in range(4)]
        for r in range(depth):
            for b in range(4):
                h_b, d_b = hs.at[b], ds.at[b]
                state[b] = row_step(h_b, d_b, h_b, d_b, cxs.at[b], cys.at[b], r, *state[b])
        return carry

    lax.fori_loop(0, ITERS, step, 0)

    bounds = slot_bounds(rows)
    slots_x = len(bounds) - 1
    totals = [sums_ref[u] for u in range(slots_x)]
    for band, first in ((0, 0), (1, rows - W)):
        slot = 0 if band == 0 else slots_x - 1
        for j in range(W):
            value = merge(lane, hs[2 * band, W + j], hs[2 * band + 1, W + j])
            edge[band * W + j] = value
            weight = done_wet[pl.ds(first + j, 1), :].astype(F32) * uplift_ref[pl.ds(first + j, 1), :] * (1.0 / BS)
            totals[slot] = totals[slot] + weight * value
    copies = [
        pltpu.make_async_copy(
            edge.at[pl.ds(band * W, W), g], out_hbm.at[pl.ds(g * rows + first, W)], sem
        )
        for band, first in ((0, 0), (1, rows - W))
        for g in range(8)
    ]
    for copy in copies:
        copy.start()

    column_bounds = slot_bounds(LANES)
    slots_y = len(column_bounds) - 1
    devices = message.shape[0]
    gauge = lax.broadcasted_iota(jnp.int32, (8, LANES), 0)
    shape = (devices, LANES)
    here = lanes_of(shape)
    per_device = 8
    home_of = jnp.where(
        here < per_device * 8,
        lax.broadcasted_iota(jnp.int32, shape, 0) * per_device + here // 8,
        -1,
    )
    built = jnp.zeros(shape, F32)
    for u in range(slots_x):
        for w in range(slots_y):
            inside = (lane >= column_bounds[w]) & (lane < column_bounds[w + 1])
            total = jnp.sum(jnp.where(inside, totals[u], 0.0), axis=1, keepdims=True)
            spread = jnp.sum(jnp.where(lane % 8 == gauge, total, 0.0), axis=0, keepdims=True)
            home = homes_ref[pl.ds(u * slots_y + w, 1), :]
            built = built + jnp.where(home_of == home, spread, 0.0)
    message[...] = built
    for copy in copies:
        copy.wait()


def final_kernel(received, gradient):
    total = jnp.sum(received[...], axis=0, keepdims=True)
    lane = lanes_of()
    row = lax.broadcasted_iota(jnp.int32, (8, LANES), 0)
    result = jnp.zeros((8, LANES), F32)
    for k in range(8):
        result = jnp.where(row == k, roll(jnp.broadcast_to(total, (8, LANES)), -8 * k), result)
    gradient[...] = result[:, :8]


def pairs(axis, first):
    return [
        pair
        for i in range(first, lax.axis_size(axis) - 1, 2)
        for pair in ((i, i + 1), (i + 1, i))
    ]


def shaped(*shape, dtype=F32):
    return jax.ShapeDtypeStruct(shape, dtype)


def bind(kernel, rows):
    def bound(*refs):
        kernel(rows, *refs)

    return bound


def body(
    terminal_elevation,
    terminal_flux_x,
    terminal_flux_y,
    courant_x,
    courant_y,
    land_sea,
    uplift,
    tile_patches,
    patch_home,
):
    gauges, rows, columns = terminal_elevation.shape
    flat = (gauges * rows, columns)
    layers = (rows + 8, gauges, columns)
    devices = lax.axis_size("gx") * lax.axis_size("gy")
    slots = tile_patches.shape[2]
    slots_x = len(slot_bounds(rows)) - 1
    vectors = payload_layout(rows)[-1] + 1
    field = pltpu.VMEM((rows, gauges, columns), F32)
    work = pltpu.VMEM(layers, F32)

    height, divergence, even_out, odd_out = pl.pallas_call(
        bind(load_kernel, rows),
        out_shape=(shaped(*layers), shaped(*layers), shaped(vectors, 8, columns), shaped(vectors, 8, columns)),
        in_specs=[HBM] * 3 + [VMEM] * 3,
        out_specs=(VMEM,) * 4,
        scratch_shapes=[field] * 3 + [pltpu.SemaphoreType.DMA((4,))],
        compiler_params=params(LOAD_MIB),
        name="load",
    )(
        terminal_elevation.reshape(flat),
        terminal_flux_x.reshape(flat),
        terminal_flux_y.reshape(flat),
        courant_x,
        courant_y,
        land_sea,
    )
    even_in = lax.ppermute(even_out, "gy", pairs("gy", 0))
    odd_in = lax.ppermute(odd_out, "gy", pairs("gy", 1))

    row_ops = rows * ITERS * 8 * columns
    center = pl.pallas_call(
        bind(center_kernel, rows),
        out_shape=shaped(*layers),
        in_specs=[VMEM] * 4,
        out_specs=VMEM,
        scratch_shapes=[work],
        compiler_params=params(8),
        cost_estimate=pl.CostEstimate(flops=row_ops * 9, bytes_accessed=2**20, transcendentals=0),
        name="center",
    )(height, divergence, courant_x, courant_y)

    x_even_out, x_odd_out = pl.pallas_call(
        bind(middle_kernel, rows),
        out_shape=(shaped(MESSAGE, 8, columns),) * 2,
        in_specs=[VMEM] * 8,
        out_specs=(VMEM,) * 2,
        compiler_params=params(4),
        name="middle",
    )(even_in, odd_in, even_out, odd_out, height, divergence, courant_x, courant_y)
    x_even_in = lax.ppermute(x_even_out, "gx", pairs("gx", 0))
    x_odd_in = lax.ppermute(x_odd_out, "gx", pairs("gx", 1))

    partial_out, bh0, bd0, cbx, cby, _, sums, homes = pl.pallas_call(
        bind(strips_kernel, rows),
        out_shape=(
            shaped(*flat), shaped(*layers), shaped(*layers), shaped(rows, columns), shaped(rows, columns),
            shaped(*layers), shaped(slots_x, 8, columns), shaped(slots, columns, dtype=jnp.int32),
        ),
        in_specs=[VMEM] * 11 + [SMEM] * 2,
        out_specs=(HBM,) + (VMEM,) * 7,
        scratch_shapes=[work, field, pltpu.SemaphoreType.DMA],
        compiler_params=params(8),
        cost_estimate=pl.CostEstimate(flops=row_ops * 9, bytes_accessed=2**20, transcendentals=0),
        name="strips",
    )(
        even_in, odd_in, even_out, odd_out, height, divergence, courant_x, courant_y, center,
        land_sea, uplift, tile_patches.reshape(-1), patch_home,
    )

    depth = 3 * W
    out, message = pl.pallas_call(
        bind(bands_kernel, rows),
        out_shape=(shaped(*flat), shaped(devices, columns)),
        in_specs=[VMEM] * 14 + [HBM],
        out_specs=(HBM, VMEM),
        input_output_aliases={14: 0},
        scratch_shapes=[
            pltpu.VMEM((4, depth + 8, 8, columns), F32),
            pltpu.VMEM((4, depth + 8, 8, columns), F32),
            pltpu.VMEM((4, depth, columns), F32),
            pltpu.VMEM((4, depth, columns), F32),
            pltpu.VMEM((2 * W, 8, columns), F32),
            pltpu.SemaphoreType.DMA,
        ],
        compiler_params=params(4),
        name="bands",
    )(
        x_even_in, x_odd_in, height, divergence, courant_x, courant_y, bh0, bd0, cbx, cby,
        land_sea, uplift, sums, homes, partial_out,
    )
    received = lax.all_to_all(message, ("gx", "gy"), 0, 0, tiled=True)
    gradient = pl.pallas_call(
        final_kernel,
        out_shape=shaped(patch_home.shape[0] // devices, gauges),
        in_specs=[VMEM],
        out_specs=VMEM,
        name="final",
    )(received)
    return (out.reshape(gauges, rows, columns), gradient)


LOAD_MIB = 8


def solution(mesh):
    in_specs = (
        P(None, "gx", "gy"),
        P(None, "gx", "gy"),
        P(None, "gx", "gy"),
        P("gx", "gy"),
        P("gx", "gy"),
        P("gx", "gy"),
        P("gx", "gy"),
        P(),
        P(),
    )
    out_specs = (P(None, "gx", "gy"), P(("gx", "gy"), None))
    return jax.shard_map(body, mesh=mesh, in_specs=in_specs, out_specs=out_specs, check_vma=False)
```

profile of v0, /device:TPU:0, one launch (start us, length us, event | category | flops | bytes accessed | tf_op | source)
XLA Modules:
  0.0 92.0 jit_solution(15877198547418900175)
XLA Ops:
  0.6 0.0 copy-start
  0.6 0.9 copy-done
  1.5 0.0 copy-start.2
  1.5 0.9 copy-done.2
  2.4 0.0 copy-start.4
  2.4 0.9 copy-done.4
  3.3 0.0 copy-start.6
  3.3 1.2 %copy-done.6 = f32[8,256,128]{2,1,0:T(8,128)S(1)} copy-done((f32[8,256,128]{2,1,0:T(8,128)S(1)}, f32[8,256,128]{2,1,0:T(8,128)}, u32[]{:S(2)}) %copy-start.6) | copy-done | bytes 1048600
  4.6 0.0 copy-start.7
  4.6 1.2 %copy-done.7 = f32[8,256,128]{2,1,0:T(8,128)S(1)} copy-done((f32[8,256,128]{2,1,0:T(8,128)S(1)}, f32[8,256,128]{2,1,0:T(8,128)}, u32[]{:S(2)}) %copy-start.7) | copy-done | bytes 1048600
  5.8 0.0 copy-start.8
  5.8 1.2 %copy-done.8 = f32[8,256,128]{2,1,0:T(8,128)S(1)} copy-done((f32[8,256,128]{2,1,0:T(8,128)S(1)}, f32[8,256,128]{2,1,0:T(8,128)}, u32[]{:S(2)}) %copy-start.8) | copy-done | bytes 1048600
  7.0 5.8 %load.1 = (f32[264,8,128]{2,1,0:T(8,128)S(1)}, f32[264,8,128]{2,1,0:T(8,128)S(1)}, f32[37,8,128]{2,1,0:T(8,128)S(1)}, f32[37,8,128]{2,1,0:T(8,128)S(1)}) custom-call(f32[2048,128]{1,0:T(8,128)S(1)} %bitcast.8, f32[2048,128]{1,0:T(8,128)S(1)} %bitcast.9, f32[2048,128]{1,0:T(8,128)S(1)} %bitcast.10, f32[256,128]{1,0:T(8,128)S(1)} %copy-done, ...), custom_call_target="tpu_custom_call" | custom-call | tf_op jit(solution)/shard_map/load/pallas_call | solution.py:470
  12.8 0.5 collective-permute-start
  13.3 0.7 collective-permute-start.1
  14.0 0.3 collective-permute-done.refs_0_
  14.3 0.0 collective-permute-done.1.refs_1_
  14.3 0.0 copy-start.11
  14.3 0.0 copy-start.1
  14.3 0.0 copy-start.3
  14.3 0.2 middle.1
  14.5 2.9 %collective-permute-start.2 = (f32[22,8,128]{2,1,0:T(8,128)S(1)}, f32[22,8,128]{2,1,0:T(8,128)S(1)}, u32[]{:S(2)}, u32[]{:S(2)}) collective-permute-start(f32[22,8,128]{2,1,0:T(8,128)S(1)} %get-tuple-element.21), channel_id=1, source_target_pairs={{0,8},{8,0},{16,24},{24,16},{1,9},{9,1},{17,25},{25,17},{2,10},{10... | collective-permute-start | bytes 270344 | tf_op jit(solution)/shard_map/ppermute | solution.py:509
  17.4 0.7 collective-permute-start.3
  18.0 0.0 copy-done.11
  18.0 0.1 reshape.24.refs_11_
  18.1 0.0 copy-done.1
  18.1 0.0 copy-done.3
  18.1 0.0 copy-start.5
  18.2 0.0 copy-start.9
  18.2 0.0 copy-start.10
  18.2 20.3 %center.1.refs_8_ = f32[264,8,128]{2,1,0:T(8,128)S(1)} custom-call(f32[264,8,128]{2,1,0:T(8,128)S(1)} %get-tuple-element.19.refs_4_.refs_0_.refs_2_, f32[264,8,128]{2,1,0:T(8,128)S(1)} %get-tuple-element.20.refs_5_.refs_1_.refs_3_, f32[256,128]{1,0:T(8,128)S(1)} %copy-done.1, f32[256,128]{1,0:T(8,128)S(1)} %copy-done.3), custom_call_target="tpu_custom_call" | custom-call | flops 18874368 | bytes 1048576 | tf_op jit(solution)/shard_map/center/pallas_call | solution.py:490
  38.5 0.0 copy-done.5
  38.5 0.0 copy-done.9
  38.5 0.0 copy-done.10
  38.5 28.4 %strips.1 = (f32[2048,128]{1,0:T(8,128)}, f32[264,8,128]{2,1,0:T(8,128)S(1)}, f32[264,8,128]{2,1,0:T(8,128)S(1)}, f32[256,128]{1,0:T(8,128)S(1)}, f32[256,128]{1...) custom-call(f32[37,8,128]{2,1,0:T(8,128)S(1)} %collective-permute-done.refs_0_, ...), custom_call_target="tpu_custom_call" | custom-call | flops 18874368 | bytes 1048576 | tf_op jit(solution)/shard_map/strips/pallas_call | solution.py:512
  67.0 0.0 collective-permute-done.2.refs_0_
  67.0 0.0 collective-permute-done.3.refs_1_
  67.0 3.9 %bands.1 = (f32[2048,128]{1,0:T(8,128)}, f32[32,128]{1,0:T(8,128)S(1)}) custom-call(f32[22,8,128]{2,1,0:T(8,128)S(1)} %collective-permute-done.2.refs_0_, f32[22,8,128]{2,1,0:T(8,128)S(1)} %collective-permute-done.3.refs_1_, f32[264,8,128]{2,1,0:T(8,128)S(1)} %get-tuple-element.19.refs_4_.refs_0_.refs_2_, ...), custom_call_target="tpu_custom_call", output_to_operand_aliasing={{0}: (14, {})} | custom-call | tf_op jit(solution)/shard_map/bands/pallas_call | solution.py:530
  71.0 19.7 %all_to_all.11 = f32[32,1,128]{2,1,0:T(1,128)} all-to-all(f32[32,1,128]{2,1,0:T(1,128)S(1)} %bitcast.11), channel_id=1, replica_groups=mesh['gx'=4,'gy'=8] {'gx','gy'}, dimensions={0} | all-to-all | bytes 32768 | tf_op jit(solution)/shard_map/all_to_all | solution.py:550
  90.6 1.4 %final.1 = f32[8,8]{1,0:T(8,128)} custom-call(f32[32,128]{1,0:T(8,128)} %bitcast.13), custom_call_target="tpu_custom_call" | custom-call | tf_op jit(solution)/shard_map/final/pallas_call | solution.py:551
Async XLA Ops:
  0.6 0.9 copy-start
  1.5 0.9 copy-start.2
  2.4 0.9 copy-start.4
  3.3 1.2 %copy-start.6 = (f32[8,256,128]{2,1,0:T(8,128)S(1)}, f32[8,256,128]{2,1,0:T(8,128)}, u32[]{:S(2)}) copy-start(f32[8,256,128]{2,1,0:T(8,128)} %param.9) | copy-start | bytes 3145732
  4.6 1.2 %copy-start.7 = (f32[8,256,128]{2,1,0:T(8,128)S(1)}, f32[8,256,128]{2,1,0:T(8,128)}, u32[]{:S(2)}) copy-start(f32[8,256,128]{2,1,0:T(8,128)} %param.10) | copy-start | bytes 3145732
  5.8 1.2 %copy-start.8 = (f32[8,256,128]{2,1,0:T(8,128)S(1)}, f32[8,256,128]{2,1,0:T(8,128)}, u32[]{:S(2)}) copy-start(f32[8,256,128]{2,1,0:T(8,128)} %param.11) | copy-start | bytes 3145732
  12.8 1.5 %collective-permute-start = (f32[37,8,128]{2,1,0:T(8,128)S(1)}, f32[37,8,128]{2,1,0:T(8,128)S(1)}, u32[]{:S(2)}, u32[]{:S(2)}) collective-permute-start(f32[37,8,128]{2,1,0:T(8,128)S(1)} %get-tuple-element.17.refs_2_), channel_id=1, source_target_pairs={{0,1},{1,0},{2,3},{3,2},{4,5},{5,4},{6,7},{7,6},{8,9},{9,8},{10,11... | collective-permute-start | bytes 454664 | tf_op jit(solution)/shard_map/ppermute | solution.py:486
  13.3 1.0 %collective-permute-start.1 = (f32[37,8,128]{2,1,0:T(8,128)S(1)}, f32[37,8,128]{2,1,0:T(8,128)S(1)}, u32[]{:S(2)}, u32[]{:S(2)}) collective-permute-start(f32[37,8,128]{2,1,0:T(8,128)S(1)} %get-tuple-element.18.refs_3_), channel_id=1, source_target_pairs={{1,2},{2,1},{3,4},{4,3},{5,6},{6,5},{9,10},{10,9},{11,12},{12,11},... | collective-permute-start | bytes 454664 | tf_op jit(solution)/shard_map/ppermute | solution.py:487
  14.3 3.7 %copy-start.11 = (s32[4,8,15]{2,1,0:T(8,128)S(1)}, s32[4,8,15]{2,1,0:T(8,128)}, u32[]{:S(2)}) copy-start(s32[4,8,15]{2,1,0:T(8,128)} %param.16) | copy-start | bytes 5764
  14.3 3.8 %copy-start.1 = (f32[256,128]{1,0:T(8,128)S(1)}, f32[256,128]{1,0:T(8,128)}, u32[]{:S(2)}) copy-start(f32[256,128]{1,0:T(8,128)} %refs_4_.3) | copy-start | bytes 393220
  14.3 3.8 %copy-start.3 = (f32[256,128]{1,0:T(8,128)S(1)}, f32[256,128]{1,0:T(8,128)}, u32[]{:S(2)}) copy-start(f32[256,128]{1,0:T(8,128)} %refs_5_.3) | copy-start | bytes 393220
  14.5 52.5 %collective-permute-start.2 = (f32[22,8,128]{2,1,0:T(8,128)S(1)}, f32[22,8,128]{2,1,0:T(8,128)S(1)}, u32[]{:S(2)}, u32[]{:S(2)}) collective-permute-start(f32[22,8,128]{2,1,0:T(8,128)S(1)} %get-tuple-element.21), channel_id=1, source_target_pairs={{0,8},{8,0},{16,24},{24,16},{1,9},{9,1},{17,25},{25,17},{2,10},{10... | collective-permute-start | bytes 270344 | tf_op jit(solution)/shard_map/ppermute | solution.py:509
  17.4 49.7 %collective-permute-start.3 = (f32[22,8,128]{2,1,0:T(8,128)S(1)}, f32[22,8,128]{2,1,0:T(8,128)S(1)}, u32[]{:S(2)}, u32[]{:S(2)}) collective-permute-start(f32[22,8,128]{2,1,0:T(8,128)S(1)} %get-tuple-element.22), channel_id=1, source_target_pairs={{8,16},{16,8},{9,17},{17,9},{10,18},{18,10},{11,19},{19,11},{12,20... | collective-permute-start | bytes 270344 | tf_op jit(solution)/shard_map/ppermute | solution.py:510
  18.1 20.4 %copy-start.5 = (s32[256,128]{1,0:T(8,128)S(1)}, s32[256,128]{1,0:T(8,128)}, u32[]{:S(2)}) copy-start(s32[256,128]{1,0:T(8,128)} %refs_10_.3) | copy-start | bytes 393220
  18.2 20.4 %copy-start.9 = (f32[256,128]{1,0:T(8,128)S(1)}, f32[256,128]{1,0:T(8,128)}, u32[]{:S(2)}) copy-start(f32[256,128]{1,0:T(8,128)} %refs_11_.1) | copy-start | bytes 393220
  18.2 20.4 %copy-start.10 = (s32[256]{0:T(256)S(1)}, s32[256]{0:T(256)}, u32[]{:S(2)}) copy-start(s32[256]{0:T(256)} %refs_12_.1) | copy-start | bytes 3076
where the time goes:
time: 92.4 us; the launch traced here: 92 us
  Pallas kernels  60 us (65%)
  blocking collectives  19.7 us (21%)
  local copies, waits for them, and re-layouts  6.51 us (7%)
  starting transfers between devices  4.7 us (5%)
    pallas_call x1, Pallas kernels, body(): pl.pallas_call(bind(strips_kernel, rows), out_shape=(shaped(*flat), shape...  28.4 us
    pallas_call x1, Pallas kernels, body(): pl.pallas_call(bind(center_kernel, rows), out_shape=shaped(*layers), in_s...  20.3 us
    all_to_all x1, blocking collectives, body(): received = lax.all_to_all(message, ('gx', 'gy'), 0, 0, tiled=True)  19.7 us
    unnamed x24, local copies, waits for them, and re-layouts  6.41 us
    pallas_call x1, Pallas kernels, body(): pl.pallas_call(bind(load_kernel, rows), out_shape=(shaped(*layers), shape...  5.75 us
    pallas_call x1, Pallas kernels, body(): pl.pallas_call(bind(bands_kernel, rows), out_shape=(shaped(*flat), shaped...  3.93 us
    ppermute x1, starting transfers between devices, body(): x_even_in = lax.ppermute(x_even_out, 'gx', pairs('gx', 0))  2.87 us
  transfers between devices with their start and end apart: 4, of which 1 were waited for; matrix products, arithmetic and copies ran while one was open for 0% of the time, Pallas kernels for 53%

commit v1 on v0

v1 whole, which is shorter than its diff:
```python
import jax
import jax.numpy as jnp
from jax import lax
from jax.experimental import pallas as pl
from jax.experimental.pallas import tpu as pltpu
from jax.sharding import PartitionSpec as P

BS = 64
ITERS = 8
LANES = 128
W = 8
GROUPS = LANES // W
F32 = jnp.float32
VMEM = pl.BlockSpec(memory_space=pltpu.VMEM)
SMEM = pl.BlockSpec(memory_space=pltpu.SMEM)
HBM = pl.BlockSpec(memory_space=pl.ANY)


def lanes_of(shape=(8, LANES)):
    return lax.broadcasted_iota(jnp.int32, shape, len(shape) - 1)


def roll(vector, distance):
    distance = distance % LANES
    return pltpu.roll(vector, distance, vector.ndim - 1) if distance else vector


def params(mebibytes):
    return pltpu.CompilerParams(vmem_limit_bytes=mebibytes * 2**20)


def tile(ref, row):
    return ref[pl.ds(row if isinstance(row, int) else pl.multiple_of(row, 8), 8), :]


def payload_layout(rows):
    heights = rows // GROUPS
    tiles = rows // 8 // GROUPS
    return (0, heights, 2 * heights, 2 * heights + tiles, 2 * heights + 2 * tiles)


def advance(items, lag):
    live = {}
    written = {}
    for i in range(-2 * lag, len(items)):
        if i + 2 * lag < len(items):
            h_in, _, _, _, _, _, r, has_above, below = items[i + 2 * lag]
            assert written.get((id(h_in), r), -(10**9)) < i
            height = h_in[r]
            live[i + 2 * lag] = [
                height,
                roll(height, LANES - 1),
                h_in[r - 1] if has_above else None,
                h_in[r + 1] if below == "row" else None,
                None,
                None,
            ]
        if 0 <= i + lag < len(items):
            state = live[i + lag]
            coef_y, r = items[i + lag][5], items[i + lag][6]
            along = coef_y[pl.ds(r, 1), :] * (state[1] - state[0])
            state[4] = along
            state[5] = roll(along, 1)
        if i >= 0:
            h_in, d_in, h_out, d_out, coef_x, _, r, has_above, below = items[i]
            height, _, above, under, along, along_before = live.pop(i)
            if below == "item":
                under = live[i + 1][0]
            if has_above:
                before = coef_x[pl.ds(r - 1, 1), :] * (height - above)
            elif i == 0 or items[i - 1][8] != "item":
                before = None
            flux = coef_x[pl.ds(r, 1), :] * ((under - height) if under is not None else -height)
            change = along - along_before + (flux if before is None else flux - before)
            divergence = d_in[r] + change
            d_out[r] = divergence
            h_out[r] = height + divergence
            written[(id(h_out), r)] = i
            before = flux


def rows_of(count, refs):
    return [refs + (r, False, "item" if r + 1 < count else None) for r in range(count)]


def run_steps(count, steps, unroll, first, then, lag):
    if first is not None:
        head = rows_of(count, first)
        for _ in range(unroll - 1):
            head = head + rows_of(count, then)
        advance(head, lag)

    def again(t, carry):
        advance(rows_of(count, then) * unroll, lag)
        return carry

    rounds = steps // unroll - (first is not None)
    if rounds == 1:
        again(0, 0)
    elif rounds:
        lax.fori_loop(0, rounds, again, 0)


def load_kernel(
    rows, h_hbm, x_hbm, y_hbm, cx_hbm, cy_hbm, wet_hbm,
    h_out, d_out, even_out, odd_out, cx_ref, cy_ref, hb, xb, yb, wet_ref, sems,
):
    gauges = 8
    parts = 4
    size = rows // parts
    plain = [
        pltpu.make_async_copy(source, target, sems.at[parts + i])
        for i, (source, target) in enumerate(((cx_hbm, cx_ref), (cy_hbm, cy_ref), (wet_hbm, wet_ref)))
    ]
    for copy in plain:
        copy.start()
    for part in range(parts):
        for source, target in ((y_hbm, yb), (x_hbm, xb), (h_hbm, hb)):
            for gauge in range(gauges):
                pltpu.make_async_copy(
                    source.at[pl.ds(gauge * rows + part * size, size)],
                    target.at[pl.ds(part * size, size), gauge],
                    sems.at[part],
                ).start()

    even = lax.rem(lax.axis_index("gy"), 2) == 0
    lane = lanes_of()
    group = lane // W
    at_h, at_d, at_cx, at_cy, at_g = payload_layout(rows)

    def put(place, to_left, to_right):
        even_out[place] = jnp.where(even, to_right, to_left)
        odd_out[place] = jnp.where(even, to_left, to_right)

    for copy in plain:
        copy.wait()
    for ref, place in ((cx_ref, at_cx), (cy_ref, at_cy)):
        for p in range(rows // 8 // GROUPS):
            to_left = to_right = jnp.zeros((8, LANES), F32)
            for k in range(GROUPS):
                value = ref[pl.ds((p * GROUPS + k) * 8, 8), :]
                to_left = jnp.where(group == k, roll(value, W * k), to_left)
                to_right = jnp.where(group == k, roll(value, W * k + W), to_right)
            put(place + p, to_left, to_right)

    state = {}

    def early(r):
        along_y = cy_ref[pl.ds(r, 1), :] * yb[r]
        state[r] = (along_y, roll(along_y, 1))

    def late(r, above, sides):
        along_y, before_y = state.pop(r)
        along_x = cx_ref[pl.ds(r, 1), :] * xb[r]
        height = wet_ref[pl.ds(r, 1), :].astype(F32) * hb[r]
        part = along_y + along_x if above is None else along_y + (along_x - above)
        divergence = part - jnp.where(lane == 0, 0.0, before_y)
        outgoing = jnp.where(lane == 0, -before_y, divergence)
        h_out[r] = height
        d_out[r] = divergence
        k = r % GROUPS
        mine = group == k
        new = (
            roll(height, W * k),
            roll(divergence, W * k),
            roll(height, W * k + W),
            roll(outgoing, W * k + W - 1),
        )
        sides = new if k == 0 else tuple(jnp.where(mine, n, s) for n, s in zip(new, sides))
        if k == GROUPS - 1:
            put(at_h + r // GROUPS, sides[0], sides[2])
            put(at_d + r // GROUPS, sides[1], sides[3])
        return along_x, sides

    above, sides = None, None
    lag = 16
    for part in range(parts):
        done = hb.at[pl.ds(0, 3 * size)]
        pltpu.make_async_copy(done, done, sems.at[part]).wait()
        low, high = part * size, (part + 1) * size
        for r in range(low - lag, high):
            if r + lag < high:
                early(r + lag)
            if r >= low:
                above, sides = late(r, above, sides)
    d_out[rows] = -above
    put(at_g, -above, roll(-above, W))


def center_first_kernel(rows, steps, h_ref, d_ref, cx_ref, cy_ref, h_out, d_out, token):
    first = (h_ref, d_ref, h_out, d_out, cx_ref, cy_ref)
    then = (h_out, d_out, h_out, d_out, cx_ref, cy_ref)
    run_steps(rows, steps, 2, first, then, 24)
    token[...] = jnp.zeros((8, LANES), F32)


def center_second_kernel(rows, steps, h_ref, d_ref, cx_ref, cy_ref, h_out, d_work):
    first = (h_ref, d_ref, h_out, d_work, cx_ref, cy_ref)
    then = (h_out, d_work, h_out, d_work, cx_ref, cy_ref)
    run_steps(rows, steps, 2, first, then, 24)


SECOND = 32


def strip(lane, own, from_left, from_right):
    return jnp.where(
        lane >= LANES - 2 * W,
        own,
        jnp.where(lane < W, from_right, jnp.where(lane < 64, from_left, roll(own, 64))),
    )


def strip_divergence(lane, own, from_left, from_right):
    middle = jnp.where(lane >= 64, roll(own, 64), 0.0) + jnp.where(
        (lane > 64 - W) & (lane <= 64), from_left, 0.0
    )
    return jnp.where(lane >= LANES - 2 * W, own, jnp.where(lane < W, from_right, middle))


def second_lanes(lane):
    return ((lane >= 16) & (lane < 40)) | ((lane >= 88) & (lane < 112))


def merge(lane, center, packed, lower):
    shift = SECOND if lower else 0
    left, right = roll(packed, 64 - shift), roll(packed, -shift)
    return jnp.where(lane < W, left, jnp.where(lane >= LANES - W, right, center))


class Sides:
    def __init__(self, even_in, odd_in, even_out, odd_out):
        self.even = lax.rem(lax.axis_index("gy"), 2) == 0
        self.lane = lanes_of()
        self.refs = (even_in, odd_in, even_out, odd_out)

    def left(self, place):
        even_in, odd_in, _, _ = self.refs
        return jnp.where(self.even, odd_in[place], even_in[place])

    def right(self, place):
        even_in, odd_in, _, _ = self.refs
        return jnp.where(self.even, even_in[place], odd_in[place])

    def right_divergence(self, place):
        _, _, even_out, odd_out = self.refs
        sent = jnp.where(self.even, even_out[place], odd_out[place])
        return self.right(place) + jnp.where(self.lane % W == 0, roll(sent, -(W - 1)), 0.0)


def middle_kernel(rows, even_in, odd_in, even_out, odd_out, h_ref, d_ref, cx_ref, cy_ref, token, x_even, x_odd):
    side = Sides(even_in, odd_in, even_out, odd_out)
    lane, group = side.lane, side.lane // W
    at_h, at_d, at_cx, at_cy, at_g = payload_layout(rows)
    last_h, last_c = rows // GROUPS - 1, rows // 8 // GROUPS - 1
    even = lax.rem(lax.axis_index("gx"), 2) == 0

    def put(place, up, down):
        x_even[place] = jnp.where(even, down, up)
        x_odd[place] = jnp.where(even, up, down)

    for j in range(W):
        put(j, h_ref[j], h_ref[rows - W + j])
        put(W + j, d_ref[j], d_ref[rows - W + j])
    first = lane < 64
    put(
        2 * W,
        jnp.where(first, side.left(at_h), roll(side.right(at_h), 64)),
        jnp.where(first, roll(side.left(at_h + last_h), 64), side.right(at_h + last_h)),
    )
    put(
        2 * W + 1,
        jnp.where(first, side.left(at_d), roll(side.right_divergence(at_d), 64)),
        jnp.where(first, roll(side.left(at_d + last_h), 64), side.right_divergence(at_d + last_h)),
    )
    put(2 * W + 2, cx_ref[0:8, :], cx_ref[rows - 8 : rows, :])
    put(2 * W + 3, cy_ref[0:8, :], cy_ref[rows - 8 : rows, :])

    def gathered(pieces):
        result = pieces[0]
        for k, piece in enumerate(pieces[1:], 1):
            result = jnp.where(group == k, roll(piece, W * k), result)
        return result

    g_left, g_right = side.left(at_g), side.right(at_g)
    put(
        2 * W + 4,
        gathered([side.left(at_cx), side.right(at_cx), side.left(at_cy), side.right(at_cy), g_left, g_right]),
        gathered(
            [roll(side.left(at_cx + last_c), W), roll(side.right(at_cx + last_c), W)]
            + [roll(side.left(at_cy + last_c), W), roll(side.right(at_cy + last_c), W)]
            + [g_left, g_right]
        ),
    )
    put(2 * W + 5, d_ref[rows], d_ref[rows])


MESSAGE = 2 * W + 6


def strips_kernel(
    rows, even_in, odd_in, even_out, odd_out, h_ref, d_ref, cx_ref, cy_ref, done_ref, wet_ref, uplift_ref, lists_ref, home_ref,
    out_hbm, bh0, bd0, cbx, cby, sums, homes, hb, db, merged, lefts, rights, sem,
):
    side = Sides(even_in, odd_in, even_out, odd_out)
    lane = side.lane
    second = second_lanes(lane)
    at_h, at_d, at_cx, at_cy, at_g = payload_layout(rows)
    count = rows // 2 + W
    offset = rows // 2 - W
    for place in range(at_g + 1):
        lefts[place] = side.left(place)
        rights[place] = side.right_divergence(place) if at_d <= place < at_cx else side.right(place)

    for ref, target, place in ((cx_ref, cbx, at_cx), (cy_ref, cby, at_cy)):

        def strip_tile(row):
            p, k = divmod(row // 8, GROUPS)
            own = ref[pl.ds(row, 8), :]
            return strip(
                lane, own, roll(lefts[place + p], 64 - W - W * k), roll(rights[place + p], -W * k)
            )

        for row in range(0, count, 8):
            target[pl.ds(row, 8), :] = jnp.where(
                second, roll(strip_tile(row + offset), SECOND), strip_tile(row)
            )

    def height_strip(row):
        m, k = divmod(row, GROUPS)
        return strip(
            lane, h_ref[row], roll(lefts[at_h + m], 64 - W - W * k), roll(rights[at_h + m], -W * k)
        )

    def divergence_strip(row):
        m, k = divmod(row, GROUPS)
        left, right = roll(lefts[at_d + m], 64 - W + 1 - W * k), roll(rights[at_d + m], -W * k)
        return strip_divergence(lane, d_ref[row], left, right)

    for row in range(count):
        bh0[row] = jnp.where(second, roll(height_strip(row + offset), SECOND), height_strip(row))
        bd0[row] = jnp.where(second, roll(divergence_strip(row + offset), SECOND), divergence_strip(row))
    bd0[count] = strip(lane, d_ref[rows], roll(lefts[at_g], 64 - W), rights[at_g])
    first = (bh0, bd0, hb, db, cbx, cby)
    then = (hb, db, hb, db, cbx, cby)
    run_steps(count, ITERS, 2, first, then, 24)

    bounds = slot_bounds(rows)
    for u in range(len(bounds) - 1):
        total = jnp.zeros((8, LANES), F32)
        for r in range(max(bounds[u], W), min(bounds[u + 1], rows - W)):
            lower = r >= rows // 2
            value = merge(lane, done_ref[r], hb[r - offset if lower else r], lower)
            merged[r] = value
            weight = wet_ref[pl.ds(r, 1), :].astype(F32) * uplift_ref[pl.ds(r, 1), :] * (1.0 / BS)
            total = total + weight * value
        sums[u] = total
    inner = rows - 2 * W
    copies = [
        pltpu.make_async_copy(merged.at[pl.ds(W, inner), g], out_hbm.at[pl.ds(g * rows + W, inner)], sem)
        for g in range(8)
    ]
    for copy in copies:
        copy.start()

    tile_at = lax.axis_index("gx") * lax.axis_size("gy") + lax.axis_index("gy")
    slots = homes.shape[0]
    for s in range(slots):
        patch = lists_ref[tile_at * slots + s]
        homes[pl.ds(s, 1), :] = jnp.full((1, LANES), home_ref[patch], jnp.int32)
    for copy in copies:
        copy.wait()


def slot_bounds(length):
    return [0] + list(range(BS // 2, length, BS)) + [length]


def bands_kernel(
    rows, x_even_in, x_odd_in, h_ref, d_ref, cx_ref, cy_ref, bh0, bd0, cbx, cby, done_wet, uplift_ref, sums_ref, homes_ref, out_in,
    out_hbm, message, hs, ds, cxs, cys, edge, sem,
):
    lane = lanes_of()
    second = second_lanes(lane)
    even = lax.rem(lax.axis_index("gx"), 2) == 0
    depth = 3 * W
    count = rows // 2 + W

    def above(place):
        return jnp.where(even, x_odd_in[place], x_even_in[place])

    def below(place):
        return jnp.where(even, x_even_in[place], x_odd_in[place])

    def both(upper, lower):
        return jnp.where(second, lower, upper)

    top, bottom, strips = 0, 1, 2
    for c, (ref, mine, packed) in enumerate(((cxs, cx_ref, cbx), (cys, cy_ref, cby))):
        halos = []
        for got in (above, below):
            value, corner = got(2 * W + 2 + c), got(2 * W + 4)
            halos.append(
                (
                    value,
                    strip(
                        lane, value, roll(corner, 64 - W - 2 * W * c), roll(corner, -W - 2 * W * c)
                    ),
                )
            )
        ref[top, 0:W, :] = halos[0][0]
        ref[top, W:depth, :] = mine[0 : 2 * W, :]
        ref[bottom, 0 : 2 * W, :] = mine[rows - 2 * W : rows, :]
        ref[bottom, 2 * W : depth, :] = halos[1][0]
        ref[strips, 0:W, :] = both(halos[0][1], packed[count - 2 * W : count - W, :])
        ref[strips, W : 2 * W, :] = both(packed[0:W, :], packed[count - W : count, :])
        ref[strips, 2 * W : depth, :] = both(packed[W : 2 * W, :], roll(halos[1][1], SECOND))

    def halo_strips(got, j):
        packed_h, packed_d = got(2 * W), got(2 * W + 1)
        return (
            strip(lane, got(j), roll(packed_h, 64 - W - W * j), roll(packed_h, -64 - W * j)),
            strip_divergence(
                lane, got(W + j), roll(packed_d, 64 - W + 1 - W * j), roll(packed_d, -64 - W * j)
            ),
        )

    flux, corner = above(2 * W + 5), above(2 * W + 4)
    flux_strip = strip(lane, flux, roll(corner, 64 - W - 4 * W), roll(corner, -5 * W))
    for j in range(W):
        upper, lower = halo_strips(above, j), halo_strips(below, j)
        h_last, d_last = roll(lower[0], SECOND), roll(lower[1], SECOND)
        d_first, d_below = bd0[j], below(W + j)
        d_top = d_ref[j]
        if j == 0:
            d_first = d_first + flux_strip
            d_top = d_top + flux
            d_below = d_below + d_ref[rows]
            d_last = d_last + roll(bd0[count], SECOND)
        hs[top, j], ds[top, j] = above(j), above(W + j)
        hs[top, W + j], ds[top, W + j] = h_ref[j], d_top
        hs[top, 2 * W + j], ds[top, 2 * W + j] = h_ref[W + j], d_ref[W + j]
        low = rows - 2 * W + j
        hs[bottom, j], ds[bottom, j] = h_ref[low], d_ref[low]
        hs[bottom, W + j], ds[bottom, W + j] = h_ref[low + W], d_ref[low + W]
        hs[bottom, 2 * W + j], ds[bottom, 2 * W + j] = below(j), d_below
        low = count - 2 * W + j
        hs[strips, j], ds[strips, j] = both(upper[0], bh0[low]), both(upper[1], bd0[low])
        hs[strips, W + j] = both(bh0[j], bh0[low + W])
        ds[strips, W + j] = both(d_first, bd0[low + W])
        hs[strips, 2 * W + j] = both(bh0[W + j], h_last)
        ds[strips, 2 * W + j] = both(bd0[W + j], d_last)

    views = [(hs.at[b], ds.at[b], hs.at[b], ds.at[b], cxs.at[b], cys.at[b]) for b in range(3)]
    items = []
    for t in range(1, ITERS + 1):
        low, high = t, depth - t
        for view in views:
            for r in range(low, high):
                items.append(view + (r, r == low, "item" if r + 1 < high else "row"))
    advance(items, 8)

    bounds = slot_bounds(rows)
    slots_x = len(bounds) - 1
    totals = [sums_ref[u] for u in range(slots_x)]
    for band, first in ((top, 0), (bottom, rows - W)):
        slot = 0 if band == top else slots_x - 1
        for j in range(W):
            value = merge(lane, hs[band, W + j], hs[strips, W + j], band == bottom)
            edge[band * W + j] = value
            weight = done_wet[pl.ds(first + j, 1), :].astype(F32) * uplift_ref[pl.ds(first + j, 1), :] * (1.0 / BS)
            totals[slot] = totals[slot] + weight * value
    copies = [
        pltpu.make_async_copy(
            edge.at[pl.ds(band * W, W), g], out_hbm.at[pl.ds(g * rows + first, W)], sem
        )
        for band, first in ((0, 0), (1, rows - W))
        for g in range(8)
    ]
    for copy in copies:
        copy.start()

    column_bounds = slot_bounds(LANES)
    slots_y = len(column_bounds) - 1
    devices = message.shape[0]
    gauge = lax.broadcasted_iota(jnp.int32, (8, LANES), 0)
    shape = (devices, LANES)
    here = lanes_of(shape)
    per_device = 8
    home_of = jnp.where(
        here < per_device * 8,
        lax.broadcasted_iota(jnp.int32, shape, 0) * per_device + here // 8,
        -1,
    )
    built = jnp.zeros(shape, F32)
    for u in range(slots_x):
        for w in range(slots_y):
            inside = (lane >= column_bounds[w]) & (lane < column_bounds[w + 1])
            total = jnp.sum(jnp.where(inside, totals[u], 0.0), axis=1, keepdims=True)
            spread = jnp.sum(jnp.where(lane % 8 == gauge, total, 0.0), axis=0, keepdims=True)
            home = homes_ref[pl.ds(u * slots_y + w, 1), :]
            built = built + jnp.where(home_of == home, spread, 0.0)
    message[...] = built
    for copy in copies:
        copy.wait()


def final_kernel(received, gradient):
    total = jnp.sum(received[...], axis=0, keepdims=True)
    lane = lanes_of()
    row = lax.broadcasted_iota(jnp.int32, (8, LANES), 0)
    result = jnp.zeros((8, LANES), F32)
    for k in range(8):
        result = jnp.where(row == k, roll(jnp.broadcast_to(total, (8, LANES)), -8 * k), result)
    gradient[...] = result[:, :8]


def pairs(axis, first):
    return [
        pair
        for i in range(first, lax.axis_size(axis) - 1, 2)
        for pair in ((i, i + 1), (i + 1, i))
    ]


def in_hbm(array):
    return pltpu.with_memory_space_constraint(array, pltpu.HBM)


def shaped(*shape, dtype=F32):
    return jax.ShapeDtypeStruct(shape, dtype)


def bind(kernel, *sizes):
    def bound(*refs):
        kernel(*sizes, *refs)

    return bound


def body(
    terminal_elevation,
    terminal_flux_x,
    terminal_flux_y,
    courant_x,
    courant_y,
    land_sea,
    uplift,
    tile_patches,
    patch_home,
):
    gauges, rows, columns = terminal_elevation.shape
    flat = (gauges * rows, columns)
    layers = (rows + 8, gauges, columns)
    devices = lax.axis_size("gx") * lax.axis_size("gy")
    slots = tile_patches.shape[2]
    slots_x = len(slot_bounds(rows)) - 1
    vectors = payload_layout(rows)[-1] + 1
    field = pltpu.VMEM((rows, gauges, columns), F32)
    work = pltpu.VMEM(layers, F32)

    height, divergence, even_out, odd_out, courant_x, courant_y = pl.pallas_call(
        bind(load_kernel, rows),
        out_shape=(
            shaped(*layers), shaped(*layers), shaped(vectors, 8, columns), shaped(vectors, 8, columns),
            shaped(rows, columns), shaped(rows, columns),
        ),
        in_specs=[HBM] * 6,
        out_specs=(VMEM,) * 6,
        scratch_shapes=[field] * 3 + [pltpu.VMEM((rows, columns), jnp.int32), pltpu.SemaphoreType.DMA((7,))],
        compiler_params=params(LOAD_MIB),
        name="load",
    )(
        in_hbm(terminal_elevation.reshape(flat)),
        in_hbm(terminal_flux_x.reshape(flat)),
        in_hbm(terminal_flux_y.reshape(flat)),
        in_hbm(courant_x),
        in_hbm(courant_y),
        in_hbm(land_sea),
    )
    even_in = lax.ppermute(even_out, "gy", pairs("gy", 0))
    odd_in = lax.ppermute(odd_out, "gy", pairs("gy", 1))

    center_h, center_d, token = pl.pallas_call(
        bind(center_first_kernel, rows, ITERS // 2),
        out_shape=(shaped(*layers), shaped(*layers), shaped(8, columns)),
        in_specs=[VMEM] * 4,
        out_specs=(VMEM,) * 3,
        compiler_params=params(4),
        cost_estimate=pl.CostEstimate(flops=COST, bytes_accessed=2**20, transcendentals=0),
        name="center_first",
    )(height, divergence, courant_x, courant_y)

    x_even_out, x_odd_out = pl.pallas_call(
        bind(middle_kernel, rows),
        out_shape=(shaped(MESSAGE, 8, columns),) * 2,
        in_specs=[VMEM] * 9,
        out_specs=(VMEM,) * 2,
        compiler_params=params(4),
        name="middle",
    )(even_in, odd_in, even_out, odd_out, height, divergence, courant_x, courant_y, token)
    x_even_in = lax.ppermute(x_even_out, "gx", pairs("gx", 0))
    x_odd_in = lax.ppermute(x_odd_out, "gx", pairs("gx", 1))

    center = pl.pallas_call(
        bind(center_second_kernel, rows, ITERS - ITERS // 2),
        out_shape=shaped(*layers),
        in_specs=[VMEM] * 4,
        out_specs=VMEM,
        scratch_shapes=[field],
        compiler_params=params(4),
        cost_estimate=pl.CostEstimate(flops=COST, bytes_accessed=2**20, transcendentals=0),
        name="center_second",
    )(center_h, center_d, courant_x, courant_y)

    count = rows // 2 + W
    packed = (count + 8, gauges, columns)
    partial_out, bh0, bd0, cbx, cby, sums, homes = pl.pallas_call(
        bind(strips_kernel, rows),
        out_shape=(
            shaped(*flat), shaped(*packed), shaped(*packed), shaped(count, columns), shaped(count, columns),
            shaped(slots_x, 8, columns), shaped(slots, columns, dtype=jnp.int32),
        ),
        in_specs=[VMEM] * 11 + [SMEM] * 2,
        out_specs=(HBM,) + (VMEM,) * 6,
        scratch_shapes=[pltpu.VMEM(packed, F32), pltpu.VMEM(packed, F32), field]
        + [pltpu.VMEM((vectors, 8, columns), F32)] * 2
        + [pltpu.SemaphoreType.DMA],
        compiler_params=params(8),
        cost_estimate=pl.CostEstimate(flops=COST, bytes_accessed=2**20, transcendentals=0),
        name="strips",
    )(
        even_in, odd_in, even_out, odd_out, height, divergence, courant_x, courant_y, center,
        land_sea, uplift, tile_patches.reshape(-1), patch_home,
    )

    depth = 3 * W
    out, message = pl.pallas_call(
        bind(bands_kernel, rows),
        out_shape=(shaped(*flat), shaped(devices, columns)),
        in_specs=[VMEM] * 14 + [HBM],
        out_specs=(HBM, VMEM),
        input_output_aliases={14: 0},
        scratch_shapes=[
            pltpu.VMEM((3, depth, 8, columns), F32),
            pltpu.VMEM((3, depth, 8, columns), F32),
            pltpu.VMEM((3, depth, columns), F32),
            pltpu.VMEM((3, depth, columns), F32),
            pltpu.VMEM((2 * W, 8, columns), F32),
            pltpu.SemaphoreType.DMA,
        ],
        compiler_params=params(4),
        name="bands",
    )(
        x_even_in, x_odd_in, height, divergence, courant_x, courant_y, bh0, bd0, cbx, cby,
        land_sea, uplift, sums, homes, partial_out,
    )
    received = lax.all_to_all(message, ("gx", "gy"), 0, 0, tiled=True)
    gradient = pl.pallas_call(
        final_kernel,
        out_shape=shaped(patch_home.shape[0] // devices, gauges),
        in_specs=[VMEM],
        out_specs=VMEM,
        name="final",
    )(received)
    return (out.reshape(gauges, rows, columns), gradient)


LOAD_MIB = 8
COST = 40_000_000


def solution(mesh):
    in_specs = (
        P(None, "gx", "gy"),
        P(None, "gx", "gy"),
        P(None, "gx", "gy"),
        P("gx", "gy"),
        P("gx", "gy"),
        P("gx", "gy"),
        P("gx", "gy"),
        P(),
        P(),
    )
    out_specs = (P(None, "gx", "gy"), P(("gx", "gy"), None))
    return jax.shard_map(body, mesh=mesh, in_specs=in_specs, out_specs=out_specs, check_vma=False)
```

time: 92.4 us -> 66.4 us (0.72)
  Pallas kernels: 60 us -> 41.4 us
  local copies, waits for them, and re-layouts: 6.51 us -> 1.4 us
  blocking collectives: 19.7 us -> 17.4 us
    pallas_call x1 -> x2, Pallas kernels: 20.3 us -> 4.73 us  [the longest x1 2.36 us: body(): pl.pallas_call(bind(center_first_kernel, rows, ITERS // 2), out_shape=(sh...]
    unnamed x24 -> x28, local copies, waits for them, and re-layouts: 6.41 us -> 1.29 us
    pallas_call x1, Pallas kernels: 5.75 us -> 2.94 us  [body(): pl.pallas_call(bind(load_kernel, rows), out_shape=(shaped(*layers), shape...]
    all_to_all x1, blocking collectives: 19.7 us -> 17.4 us  [body(): received = lax.all_to_all(message, ('gx', 'gy'), 0, 0, tiled=True)]
  transfers between devices with their start and end apart: 4 -> 4, of which waited for: 1 -> 0; matrix products, arithmetic and copies ran while one was open for 0% -> 0% of each run, Pallas kernels for 53% -> 49%
where the time goes in v1:
time: 66.4 us; the launch traced here: 66.1 us
  Pallas kernels  41.4 us (62%)
  blocking collectives  17.4 us (26%)
  starting transfers between devices  5.04 us (8%)
  local copies, waits for them, and re-layouts  1.4 us (2%)
  between operations  0.87 us (1%)
    pallas_call x1, Pallas kernels, body(): pl.pallas_call(bind(strips_kernel, rows), out_shape=(shaped(*flat), shape...  27.6 us
    all_to_all x1, blocking collectives, body(): received = lax.all_to_all(message, ('gx', 'gy'), 0, 0, tiled=True)  17.4 us
    pallas_call x1, Pallas kernels, body(): pl.pallas_call(bind(bands_kernel, rows), out_shape=(shaped(*flat), shaped...  3.65 us
    pallas_call x1, Pallas kernels, body(): pl.pallas_call(bind(load_kernel, rows), out_shape=(shaped(*layers), shape...  2.94 us
    ppermute x1, starting transfers between devices, body(): x_even_in = lax.ppermute(x_even_out, 'gx', pairs('gx', 0))  2.58 us
    pallas_call x1, Pallas kernels, body(): pl.pallas_call(bind(center_first_kernel, rows, ITERS // 2), out_shape=(sh...  2.36 us
    pallas_call x1, Pallas kernels, body(): pl.pallas_call(bind(center_second_kernel, rows, ITERS - ITERS // 2), out_...  2.36 us
    pallas_call x1, Pallas kernels, body(): pl.pallas_call(final_kernel, out_shape=shaped(patch_home.shape[0] // devi...  1.39 us
  transfers between devices with their start and end apart: 4, of which 0 were waited for; matrix products, arithmetic and copies ran while one was open for 0% of the time, Pallas kernels for 49%

profile of v1, /device:TPU:0, one launch (start us, length us, event | category | flops | bytes accessed | tf_op | source)
XLA Modules:
  0.0 66.1 jit_solution(6604413780144460551)
XLA Ops:
  0.6 2.9 %load.1 = (f32[264,8,128]{2,1,0:T(8,128)S(1)}, f32[264,8,128]{2,1,0:T(8,128)S(1)}, f32[37,8,128]{2,1,0:T(8,128)S(1)}, f32[37,8,128]{2,1,0:T(8,128)S(1)}, f32[256,128]{1,0:T(8,128)S(1)}, /*index=5*/f32[256,128]{1,0:T(8,128)S(1)}) custom-call(f32[2048,128]{1,0:T(8,128)} %bitcast.9, f32[2048,128]{1,0:T(8,128)} %bitcast.10, f32[2048,128]{1,0:T(8,128)} %bitcast.11, ...), custom_call_target="tpu_custom_call" | custom-call | tf_op jit(solution)/shard_map/load/pallas_call | solution.py:562
  3.6 0.0 copy-start.3
  3.6 0.0 copy-start.5
  3.6 0.5 collective-permute-start
  4.1 0.7 collective-permute-start.1
  4.8 2.4 %center_first.1 = (f32[264,8,128]{2,1,0:T(8,128)S(1)}, f32[264,8,128]{2,1,0:T(8,128)S(1)}, f32[8,128]{1,0:T(8,128)S(1)}) custom-call(f32[264,8,128]{2,1,0:T(8,128)S(1)} %get-tuple-element.24.refs_0_.refs_4_.refs_2_, f32[264,8,128]{2,1,0:T(8,128)S(1)} %get-tuple-element.25.refs_1_.refs_5_.refs_3_, f32[256,128]{1,0:T(8,128)S(1)} %get-tuple-element.26.refs_2_.refs_6_.refs_4_, ...), custom_call_target="tpu_custom_call" | custom-call | flops 40000000 | bytes 1048576 | tf_op jit(solution)/shard_map/center_first/pallas_call | solution.py:584
  7.2 0.0 copy-start.1
  7.2 0.0 collective-permute-done.refs_0_
  7.2 0.0 copy-start.7
  7.2 0.0 collective-permute-done.1.refs_1_
  7.2 0.0 copy-start.9
  7.2 0.0 copy-done.3
  7.2 0.0 copy-done.5
  7.2 0.0 copy-start.13
  7.2 1.1 %middle.1 = (f32[22,8,128]{2,1,0:T(8,128)}, f32[22,8,128]{2,1,0:T(8,128)}) custom-call(f32[37,8,128]{2,1,0:T(8,128)S(1)} %collective-permute-done.refs_0_, f32[37,8,128]{2,1,0:T(8,128)S(1)} %collective-permute-done.1.refs_1_, f32[37,8,128]{2,1,0:T(8,128)S(1)} %get-tuple-element.22.refs_2_, f32[37,8,128]{2,1,0:T(8,128)S(1)} %get-tuple-element.23.refs_3_, ...), custom_call_target="tpu_custom_call" | custom-call | tf_op jit(solution)/shard_map/middle/pallas_call | solution.py:594
  8.3 0.0 copy-done.1
  8.3 0.0 copy-done.7
  8.3 0.0 copy-done.9
  8.3 2.6 %collective-permute-start.2 = (f32[22,8,128]{2,1,0:T(8,128)}, f32[22,8,128]{2,1,0:T(8,128)}, u32[]{:S(2)}, u32[]{:S(2)}) collective-permute-start(f32[22,8,128]{2,1,0:T(8,128)} %get-tuple-element.29), channel_id=1, source_target_pairs={{0,8},{8,0},{16,24},{24,16},{1,9},{9,1},{17,25},{25,17},{2,10},{10... | collective-permute-start | bytes 270344 | tf_op jit(solution)/shard_map/ppermute | solution.py:602
  10.9 1.3 %collective-permute-start.3 = (f32[22,8,128]{2,1,0:T(8,128)}, f32[22,8,128]{2,1,0:T(8,128)}, u32[]{:S(2)}, u32[]{:S(2)}) collective-permute-start(f32[22,8,128]{2,1,0:T(8,128)} %get-tuple-element.30), channel_id=1, source_target_pairs={{8,16},{16,8},{9,17},{17,9},{10,18},{18,10},{11,19},{19,11},{12,20... | collective-permute-start | bytes 270344 | tf_op jit(solution)/shard_map/ppermute | solution.py:603
  12.2 0.0 copy-done.13
  12.2 0.1 reshape.24.refs_11_
  12.3 0.0 copy-start.2
  12.3 1.2 %copy-done.2 = f32[264,8,128]{2,1,0:T(8,128)S(1)} copy-done((f32[264,8,128]{2,1,0:T(8,128)S(1)}, f32[264,8,128]{2,1,0:T(8,128)}, u32[]{:S(2)}) %copy-start.2) | copy-done | bytes 1081368
  13.5 0.0 copy-start
  13.5 0.0 copy-start.4
  13.5 0.0 copy-start.6
  13.5 0.0 copy-start.8
  13.5 0.0 copy-start.10
  13.5 0.0 copy-start.11
  13.5 0.0 copy-start.12
  13.6 2.4 %center_second.1.refs_8_ = f32[264,8,128]{2,1,0:T(8,128)S(1)} custom-call(f32[264,8,128]{2,1,0:T(8,128)S(1)} %get-tuple-element.31.refs_0_, f32[264,8,128]{2,1,0:T(8,128)S(1)} %copy-done.2, f32[256,128]{1,0:T(8,128)S(1)} %get-tuple-element.26.refs_2_.refs_6_.refs_4_, f32[256,128]{1,0:T(8,128)S(1)} %get-tuple-element.27.refs_3_.refs_7_.refs_5_), custom_call_target="tpu_custom_call" | custom-call | flops 40000000 | bytes 1048576 | tf_op jit(solution)/shard_map/center_second/pallas_call | solution.py:605
  15.9 0.0 copy-done
  15.9 0.0 copy-done.4
  15.9 0.0 copy-done.6
  16.0 0.0 copy-done.8
  16.0 0.0 copy-done.10
  16.0 0.0 copy-done.11
  16.0 0.0 copy-done.12
  16.0 27.6 %strips.1 = (f32[2048,128]{1,0:T(8,128)}, f32[144,8,128]{2,1,0:T(8,128)S(1)}, f32[144,8,128]{2,1,0:T(8,128)S(1)}, f32[136,128]{1,0:T(8,128)S(1)}, f32[136,128]{1...) custom-call(f32[37,8,128]{2,1,0:T(8,128)S(1)} %copy-done.8, f32[37,8,128]{2,1,0:T(8,128)S(1)} %copy-done.10, ...), custom_call_target="tpu_custom_call" | custom-call | flops 40000000 | bytes 1048576 | tf_op jit(solution)/shard_map/strips/pallas_call | solution.py:618
  43.6 0.0 collective-permute-done.2.refs_0_
  43.6 0.0 collective-permute-done.3.refs_1_
  43.6 3.6 %bands.1 = (f32[2048,128]{1,0:T(8,128)}, f32[32,128]{1,0:T(8,128)S(1)}) custom-call(f32[22,8,128]{2,1,0:T(8,128)} %collective-permute-done.2.refs_0_, f32[22,8,128]{2,1,0:T(8,128)} %collective-permute-done.3.refs_1_, f32[264,8,128]{2,1,0:T(8,128)S(1)} %get-tuple-element.24.refs_0_.refs_4_.refs_2_, ...), custom_call_target="tpu_custom_call", output_to_operand_aliasing={{0}: (14, {})} | custom-call | tf_op jit(solution)/shard_map/bands/pallas_call | solution.py:638
  47.3 17.4 %all_to_all.11 = f32[32,1,128]{2,1,0:T(1,128)} all-to-all(f32[32,1,128]{2,1,0:T(1,128)S(1)} %bitcast.8), channel_id=1, replica_groups=mesh['gx'=4,'gy'=8] {'gx','gy'}, dimensions={0} | all-to-all | bytes 32768 | tf_op jit(solution)/shard_map/all_to_all | solution.py:658
  64.7 1.4 %final.1 = f32[8,8]{1,0:T(8,128)} custom-call(f32[32,128]{1,0:T(8,128)} %bitcast.13), custom_call_target="tpu_custom_call" | custom-call | tf_op jit(solution)/shard_map/final/pallas_call | solution.py:659
Async XLA Ops:
  3.6 3.6 %copy-start.3 = (f32[37,8,128]{2,1,0:T(8,128)}, f32[37,8,128]{2,1,0:T(8,128)S(1)}, u32[]{:S(2)}) copy-start(f32[37,8,128]{2,1,0:T(8,128)S(1)} %get-tuple-element.22.refs_2_) | copy-start | bytes 454660
  3.6 3.6 %copy-start.5 = (f32[37,8,128]{2,1,0:T(8,128)}, f32[37,8,128]{2,1,0:T(8,128)S(1)}, u32[]{:S(2)}) copy-start(f32[37,8,128]{2,1,0:T(8,128)S(1)} %get-tuple-element.23.refs_3_) | copy-start | bytes 454660
  3.6 3.6 %collective-permute-start = (f32[37,8,128]{2,1,0:T(8,128)S(1)}, f32[37,8,128]{2,1,0:T(8,128)S(1)}, u32[]{:S(2)}, u32[]{:S(2)}) collective-permute-start(f32[37,8,128]{2,1,0:T(8,128)S(1)} %get-tuple-element.22.refs_2_), channel_id=1, source_target_pairs={{0,1},{1,0},{2,3},{3,2},{4,5},{5,4},{6,7},{7,6},{8,9},{9,8},{10,11... | collective-permute-start | bytes 454664 | tf_op jit(solution)/shard_map/ppermute | solution.py:581
  4.1 3.1 %collective-permute-start.1 = (f32[37,8,128]{2,1,0:T(8,128)S(1)}, f32[37,8,128]{2,1,0:T(8,128)S(1)}, u32[]{:S(2)}, u32[]{:S(2)}) collective-permute-start(f32[37,8,128]{2,1,0:T(8,128)S(1)} %get-tuple-element.23.refs_3_), channel_id=1, source_target_pairs={{1,2},{2,1},{3,4},{4,3},{5,6},{6,5},{9,10},{10,9},{11,12},{12,11},... | collective-permute-start | bytes 454664 | tf_op jit(solution)/shard_map/ppermute | solution.py:582
  7.2 1.1 %copy-start.1 = (f32[264,8,128]{2,1,0:T(8,128)}, f32[264,8,128]{2,1,0:T(8,128)S(1)}, u32[]{:S(2)}) copy-start(f32[264,8,128]{2,1,0:T(8,128)S(1)} %get-tuple-element.32.refs_1_) | copy-start | bytes 3244036
  7.2 1.1 %copy-start.7 = (f32[37,8,128]{2,1,0:T(8,128)}, f32[37,8,128]{2,1,0:T(8,128)S(1)}, u32[]{:S(2)}) copy-start(f32[37,8,128]{2,1,0:T(8,128)S(1)} %collective-permute-done.refs_0_) | copy-start | bytes 454660
  7.2 1.1 %copy-start.9 = (f32[37,8,128]{2,1,0:T(8,128)}, f32[37,8,128]{2,1,0:T(8,128)S(1)}, u32[]{:S(2)}) copy-start(f32[37,8,128]{2,1,0:T(8,128)S(1)} %collective-permute-done.1.refs_1_) | copy-start | bytes 454660
  7.2 4.9 %copy-start.13 = (s32[4,8,15]{2,1,0:T(8,128)S(1)}, s32[4,8,15]{2,1,0:T(8,128)}, u32[]{:S(2)}) copy-start(s32[4,8,15]{2,1,0:T(8,128)} %param.16) | copy-start | bytes 5764
  8.3 35.3 %collective-permute-start.2 = (f32[22,8,128]{2,1,0:T(8,128)}, f32[22,8,128]{2,1,0:T(8,128)}, u32[]{:S(2)}, u32[]{:S(2)}) collective-permute-start(f32[22,8,128]{2,1,0:T(8,128)} %get-tuple-element.29), channel_id=1, source_target_pairs={{0,8},{8,0},{16,24},{24,16},{1,9},{9,1},{17,25},{25,17},{2,10},{10... | collective-permute-start | bytes 270344 | tf_op jit(solution)/shard_map/ppermute | solution.py:602
  10.9 32.7 %collective-permute-start.3 = (f32[22,8,128]{2,1,0:T(8,128)}, f32[22,8,128]{2,1,0:T(8,128)}, u32[]{:S(2)}, u32[]{:S(2)}) collective-permute-start(f32[22,8,128]{2,1,0:T(8,128)} %get-tuple-element.30), channel_id=1, source_target_pairs={{8,16},{16,8},{9,17},{17,9},{10,18},{18,10},{11,19},{19,11},{12,20... | collective-permute-start | bytes 270344 | tf_op jit(solution)/shard_map/ppermute | solution.py:603
  12.3 1.2 %copy-start.2 = (f32[264,8,128]{2,1,0:T(8,128)S(1)}, f32[264,8,128]{2,1,0:T(8,128)}, u32[]{:S(2)}) copy-start(f32[264,8,128]{2,1,0:T(8,128)} %copy-done.1) | copy-start | bytes 3244036
  13.5 2.4 %copy-start = (s32[256,128]{1,0:T(8,128)S(1)}, s32[256,128]{1,0:T(8,128)}, u32[]{:S(2)}) copy-start(s32[256,128]{1,0:T(8,128)} %refs_10_.3) | copy-start | bytes 393220
  13.5 2.4 %copy-start.4 = (f32[37,8,128]{2,1,0:T(8,128)S(1)}, f32[37,8,128]{2,1,0:T(8,128)}, u32[]{:S(2)}) copy-start(f32[37,8,128]{2,1,0:T(8,128)} %copy-done.3) | copy-start | bytes 454660
  13.5 2.4 %copy-start.6 = (f32[37,8,128]{2,1,0:T(8,128)S(1)}, f32[37,8,128]{2,1,0:T(8,128)}, u32[]{:S(2)}) copy-start(f32[37,8,128]{2,1,0:T(8,128)} %copy-done.5) | copy-start | bytes 454660
  13.5 2.4 %copy-start.8 = (f32[37,8,128]{2,1,0:T(8,128)S(1)}, f32[37,8,128]{2,1,0:T(8,128)}, u32[]{:S(2)}) copy-start(f32[37,8,128]{2,1,0:T(8,128)} %copy-done.7) | copy-start | bytes 454660
  13.5 2.4 %copy-start.10 = (f32[37,8,128]{2,1,0:T(8,128)S(1)}, f32[37,8,128]{2,1,0:T(8,128)}, u32[]{:S(2)}) copy-start(f32[37,8,128]{2,1,0:T(8,128)} %copy-done.9) | copy-start | bytes 454660
  13.5 2.4 %copy-start.11 = (f32[256,128]{1,0:T(8,128)S(1)}, f32[256,128]{1,0:T(8,128)}, u32[]{:S(2)}) copy-start(f32[256,128]{1,0:T(8,128)} %refs_11_.1) | copy-start | bytes 393220
  13.5 2.4 %copy-start.12 = (s32[256]{0:T(256)S(1)}, s32[256]{0:T(256)}, u32[]{:S(2)}) copy-start(s32[256]{0:T(256)} %refs_12_.1) | copy-start | bytes 3076

commit v2 on v1

--- a/solution.py
+++ b/solution.py
@@ -79,6 +79,21 @@
             before = flux
 
 
+class Stores:
+    def __init__(self, lag):
+        self.lag, self.waiting = lag, []
+
+    def __call__(self, ref, place, value):
+        self.waiting.append((ref, place, value))
+        if len(self.waiting) > self.lag:
+            self.release(1)
+
+    def release(self, count=None):
+        for ref, place, value in self.waiting[:count]:
+            ref[place] = value
+        self.waiting = self.waiting[count:] if count else []
+
+
 def rows_of(count, refs):
     return [refs + (r, False, "item" if r + 1 < count else None) for r in range(count)]
 
@@ -194,28 +209,29 @@
     token[...] = jnp.zeros((8, LANES), F32)
 
 
-def center_second_kernel(rows, steps, h_ref, d_ref, cx_ref, cy_ref, h_out, d_work):
-    first = (h_ref, d_ref, h_out, d_work, cx_ref, cy_ref)
-    then = (h_out, d_work, h_out, d_work, cx_ref, cy_ref)
-    run_steps(rows, steps, 2, first, then, 24)
+def center_second_kernel(rows, steps, h_in, d_in, cx_ref, cy_ref, h_out, d_out):
+    then = (h_out, d_out, h_out, d_out, cx_ref, cy_ref)
+    run_steps(rows, steps, 2, None, then, 24)
 
 
 SECOND = 32
 
 
-def strip(lane, own, from_left, from_right):
+def strip(lane, own, from_left, from_right, shift=0):
+    at = (lane - shift) % LANES
     return jnp.where(
-        lane >= LANES - 2 * W,
-        own,
-        jnp.where(lane < W, from_right, jnp.where(lane < 64, from_left, roll(own, 64))),
-    )
-
-
-def strip_divergence(lane, own, from_left, from_right):
-    middle = jnp.where(lane >= 64, roll(own, 64), 0.0) + jnp.where(
-        (lane > 64 - W) & (lane <= 64), from_left, 0.0
-    )
-    return jnp.where(lane >= LANES - 2 * W, own, jnp.where(lane < W, from_right, middle))
+        at >= LANES - 2 * W,
+        roll(own, shift),
+        jnp.where(at < W, from_right, jnp.where(at < 64, from_left, roll(own, 64 + shift))),
+    )
+
+
+def strip_divergence(lane, own, from_left, from_right, shift=0):
+    at = (lane - shift) % LANES
+    middle = jnp.where(at >= 64, roll(own, 64 + shift), 0.0) + jnp.where(
+        (at > 64 - W) & (at <= 64), from_left, 0.0
+    )
+    return jnp.where(at >= LANES - 2 * W, roll(own, shift), jnp.where(at < W, from_right, middle))
 
 
 def second_lanes(lane):
@@ -254,10 +270,11 @@
     at_h, at_d, at_cx, at_cy, at_g = payload_layout(rows)
     last_h, last_c = rows // GROUPS - 1, rows // 8 // GROUPS - 1
     even = lax.rem(lax.axis_index("gx"), 2) == 0
+    store = Stores(24)
 
     def put(place, up, down):
-        x_even[place] = jnp.where(even, down, up)
-        x_odd[place] = jnp.where(even, up, down)
+        store(x_even, place, jnp.where(even, down, up))
+        store(x_odd, place, jnp.where(even, up, down))
 
     for j in range(W):
         put(j, h_ref[j], h_ref[rows - W + j])
@@ -293,6 +310,7 @@
         ),
     )
     put(2 * W + 5, d_ref[rows], d_ref[rows])
+    store.release()
 
 
 MESSAGE = 2 * W + 6
@@ -300,7 +318,7 @@
 
 def strips_kernel(
     rows, even_in, odd_in, even_out, odd_out, h_ref, d_ref, cx_ref, cy_ref, done_ref, wet_ref, uplift_ref, lists_ref, home_ref,
-    out_hbm, bh0, bd0, cbx, cby, sums, homes, hb, db, merged, lefts, rights, sem,
+    merged, bh0, bd0, cbx, cby, sums, homes, hb, db, lefts, rights,
 ):
     side = Sides(even_in, odd_in, even_out, odd_out)
     lane = side.lane
@@ -308,38 +326,49 @@
     at_h, at_d, at_cx, at_cy, at_g = payload_layout(rows)
     count = rows // 2 + W
     offset = rows // 2 - W
+    store = Stores(24)
     for place in range(at_g + 1):
-        lefts[place] = side.left(place)
-        rights[place] = side.right_divergence(place) if at_d <= place < at_cx else side.right(place)
+        store(lefts, place, side.left(place))
+        right = side.right_divergence(place) if at_d <= place < at_cx else side.right(place)
+        store(rights, place, right)
+    store.release()
 
     for ref, target, place in ((cx_ref, cbx, at_cx), (cy_ref, cby, at_cy)):
 
-        def strip_tile(row):
+        def strip_tile(row, shift):
             p, k = divmod(row // 8, GROUPS)
-            own = ref[pl.ds(row, 8), :]
-            return strip(
-                lane, own, roll(lefts[place + p], 64 - W - W * k), roll(rights[place + p], -W * k)
-            )
+            left = roll(lefts[place + p], 64 - W - W * k + shift)
+            right = roll(rights[place + p], shift - W * k)
+            return strip(lane, ref[pl.ds(row, 8), :], left, right, shift)
 
         for row in range(0, count, 8):
-            target[pl.ds(row, 8), :] = jnp.where(
-                second, roll(strip_tile(row + offset), SECOND), strip_tile(row)
-            )
-
-    def height_strip(row):
-        m, k = divmod(row, GROUPS)
-        return strip(
-            lane, h_ref[row], roll(lefts[at_h + m], 64 - W - W * k), roll(rights[at_h + m], -W * k)
-        )
-
-    def divergence_strip(row):
-        m, k = divmod(row, GROUPS)
-        left, right = roll(lefts[at_d + m], 64 - W + 1 - W * k), roll(rights[at_d + m], -W * k)
-        return strip_divergence(lane, d_ref[row], left, right)
-
-    for row in range(count):
-        bh0[row] = jnp.where(second, roll(height_strip(row + offset), SECOND), height_strip(row))
-        bd0[row] = jnp.where(second, roll(divergence_strip(row + offset), SECOND), divergence_strip(row))
+            value = jnp.where(second, strip_tile(row + offset, SECOND), strip_tile(row, 0))
+            store(target, pl.ds(row, 8), value)
+
+    def strips_at(row, m, k, shift):
+        left, right = lefts[at_h + m], rights[at_h + m]
+        left, right = roll(left, 64 - W - W * k + shift), roll(right, shift - W * k)
+        height = strip(lane, h_ref[row], left, right, shift)
+        left, right = lefts[at_d + m], rights[at_d + m]
+        left, right = roll(left, 64 - W + 1 - W * k + shift), roll(right, shift - W * k)
+        return height, strip_divergence(lane, d_ref[row], left, right, shift)
+
+    def build(b, length):
+        values = []
+        for k in range(length):
+            row = b * GROUPS + k
+            upper = strips_at(row, b, k, 0)
+            lower_m, lower_k = divmod(offset + k, GROUPS)
+            lower = strips_at(row + offset, b + lower_m, lower_k, SECOND)
+            values.append([jnp.where(second, low, up) for up, low in zip(upper, lower)])
+        for k in range(length):
+            bh0[b * GROUPS + k], bd0[b * GROUPS + k] = values[k]
+        return length
+
+    lax.fori_loop(0, count // GROUPS, lambda b, carry: build(b, GROUPS) and carry, 0)
+    if count % GROUPS:
+        build(count // GROUPS, count % GROUPS)
+    store.release()
     bd0[count] = strip(lane, d_ref[rows], roll(lefts[at_g], 64 - W), rights[at_g])
     first = (bh0, bd0, hb, db, cbx, cby)
     then = (hb, db, hb, db, cbx, cby)
@@ -351,35 +380,35 @@
         for r in range(max(bounds[u], W), min(bounds[u + 1], rows - W)):
             lower = r >= rows // 2
             value = merge(lane, done_ref[r], hb[r - offset if lower else r], lower)
-            merged[r] = value
+            store(merged, r, value)
             weight = wet_ref[pl.ds(r, 1), :].astype(F32) * uplift_ref[pl.ds(r, 1), :] * (1.0 / BS)
             total = total + weight * value
-        sums[u] = total
+        store(sums, u, total)
+    store.release()
+    tile_row, tile_column = lax.axis_index("gx"), lax.axis_index("gy")
+    slots = homes.shape[0]
+    for s in range(slots):
+        patch = lists_ref[tile_row, tile_column, s]
+        homes[pl.ds(s, 1), :] = jnp.full((1, LANES), home_ref[patch], jnp.int32)
+
+
+def slot_bounds(length):
+    return [0] + list(range(BS // 2, length, BS)) + [length]
+
+
+def bands_kernel(
+    rows, x_even_in, x_odd_in, h_ref, d_ref, cx_ref, cy_ref, bh0, bd0, cbx, cby, done_wet, uplift_ref, sums_ref, homes_ref, merged,
+    out_hbm, message, hs, ds, cxs, cys, edge, sems,
+):
     inner = rows - 2 * W
     copies = [
-        pltpu.make_async_copy(merged.at[pl.ds(W, inner), g], out_hbm.at[pl.ds(g * rows + W, inner)], sem)
+        pltpu.make_async_copy(
+            merged.at[pl.ds(W, inner), g], out_hbm.at[pl.ds(g * rows + W, inner)], sems.at[g]
+        )
         for g in range(8)
     ]
     for copy in copies:
         copy.start()
-
-    tile_at = lax.axis_index("gx") * lax.axis_size("gy") + lax.axis_index("gy")
-    slots = homes.shape[0]
-    for s in range(slots):
-        patch = lists_ref[tile_at * slots + s]
-        homes[pl.ds(s, 1), :] = jnp.full((1, LANES), home_ref[patch], jnp.int32)
-    for copy in copies:
-        copy.wait()
-
-
-def slot_bounds(length):
-    return [0] + list(range(BS // 2, length, BS)) + [length]
-
-
-def bands_kernel(
-    rows, x_even_in, x_odd_in, h_ref, d_ref, cx_ref, cy_ref, bh0, bd0, cbx, cby, done_wet, uplift_ref, sums_ref, homes_ref, out_in,
-    out_hbm, message, hs, ds, cxs, cys, edge, sem,
-):
     lane = lanes_of()
     second = second_lanes(lane)
     even = lax.rem(lax.axis_index("gx"), 2) == 0
@@ -394,6 +423,8 @@
 
     def both(upper, lower):
         return jnp.where(second, lower, upper)
+
+    store = Stores(24)
 
     top, bottom, strips = 0, 1, 2
     for c, (ref, mine, packed) in enumerate(((cxs, cx_ref, cbx), (cys, cy_ref, cby))):
@@ -408,13 +439,15 @@
                     ),
                 )
             )
-        ref[top, 0:W, :] = halos[0][0]
-        ref[top, W:depth, :] = mine[0 : 2 * W, :]
-        ref[bottom, 0 : 2 * W, :] = mine[rows - 2 * W : rows, :]
-        ref[bottom, 2 * W : depth, :] = halos[1][0]
-        ref[strips, 0:W, :] = both(halos[0][1], packed[count - 2 * W : count - W, :])
-        ref[strips, W : 2 * W, :] = both(packed[0:W, :], packed[count - W : count, :])
-        ref[strips, 2 * W : depth, :] = both(packed[W : 2 * W, :], roll(halos[1][1], SECOND))
+        store(ref, (top, slice(0, W)), halos[0][0])
+        store(ref, (top, slice(W, depth)), mine[0 : 2 * W, :])
+        store(ref, (bottom, slice(0, 2 * W)), mine[rows - 2 * W : rows, :])
+        store(ref, (bottom, slice(2 * W, depth)), halos[1][0])
+        store(ref, (strips, slice(0, W)), both(halos[0][1], packed[count - 2 * W : count - W, :]))
+        store(ref, (strips, slice(W, 2 * W)), both(packed[0:W, :], packed[count - W : count, :]))
+        store(
+            ref, (strips, slice(2 * W, depth)), both(packed[W : 2 * W, :], roll(halos[1][1], SECOND))
+        )
 
     def halo_strips(got, j):
         packed_h, packed_d = got(2 * W), got(2 * W + 1)
@@ -437,19 +470,21 @@
             d_top = d_top + flux
             d_below = d_below + d_ref[rows]
             d_last = d_last + roll(bd0[count], SECOND)
-        hs[top, j], ds[top, j] = above(j), above(W + j)
-        hs[top, W + j], ds[top, W + j] = h_ref[j], d_top
-        hs[top, 2 * W + j], ds[top, 2 * W + j] = h_ref[W + j], d_ref[W + j]
-        low = rows - 2 * W + j
-        hs[bottom, j], ds[bottom, j] = h_ref[low], d_ref[low]
-        hs[bottom, W + j], ds[bottom, W + j] = h_ref[low + W], d_ref[low + W]
-        hs[bottom, 2 * W + j], ds[bottom, 2 * W + j] = below(j), d_below
-        low = count - 2 * W + j
-        hs[strips, j], ds[strips, j] = both(upper[0], bh0[low]), both(upper[1], bd0[low])
-        hs[strips, W + j] = both(bh0[j], bh0[low + W])
-        ds[strips, W + j] = both(d_first, bd0[low + W])
-        hs[strips, 2 * W + j] = both(bh0[W + j], h_last)
-        ds[strips, 2 * W + j] = both(bd0[W + j], d_last)
+        low, packed_low = rows - 2 * W + j, count - 2 * W + j
+        for band, place, height, divergence in (
+            (top, j, above(j), above(W + j)),
+            (top, W + j, h_ref[j], d_top),
+            (top, 2 * W + j, h_ref[W + j], d_ref[W + j]),
+            (bottom, j, h_ref[low], d_ref[low]),
+            (bottom, W + j, h_ref[low + W], d_ref[low + W]),
+            (bottom, 2 * W + j, below(j), d_below),
+            (strips, j, both(upper[0], bh0[packed_low]), both(upper[1], bd0[packed_low])),
+            (strips, W + j, both(bh0[j], bh0[packed_low + W]), both(d_first, bd0[packed_low + W])),
+            (strips, 2 * W + j, both(bh0[W + j], h_last), both(bd0[W + j], d_last)),
+        ):
+            store(hs, (band, place), height)
+            store(ds, (band, place), divergence)
+    store.release()
 
     views = [(hs.at[b], ds.at[b], hs.at[b], ds.at[b], cxs.at[b], cys.at[b]) for b in range(3)]
     items = []
@@ -467,17 +502,20 @@
         slot = 0 if band == top else slots_x - 1
         for j in range(W):
             value = merge(lane, hs[band, W + j], hs[strips, W + j], band == bottom)
-            edge[band * W + j] = value
+            store(edge, band * W + j, value)
             weight = done_wet[pl.ds(first + j, 1), :].astype(F32) * uplift_ref[pl.ds(first + j, 1), :] * (1.0 / BS)
             totals[slot] = totals[slot] + weight * value
-    copies = [
+    store.release()
+    edges = [
         pltpu.make_async_copy(
-            edge.at[pl.ds(band * W, W), g], out_hbm.at[pl.ds(g * rows + first, W)], sem
+            edge.at[pl.ds(band * W, W), g],
+            out_hbm.at[pl.ds(g * rows + first, W)],
+            sems.at[8 + 8 * band + g],
         )
         for band, first in ((0, 0), (1, rows - W))
         for g in range(8)
     ]
-    for copy in copies:
+    for copy in edges:
         copy.start()
 
     column_bounds = slot_bounds(LANES)
@@ -501,7 +539,7 @@
             home = homes_ref[pl.ds(u * slots_y + w, 1), :]
             built = built + jnp.where(home_of == home, spread, 0.0)
     message[...] = built
-    for copy in copies:
+    for copy in copies + edges:
         copy.wait()
 
 
@@ -521,6 +559,10 @@
         for i in range(first, lax.axis_size(axis) - 1, 2)
         for pair in ((i, i + 1), (i + 1, i))
     ]
+
+
+def in_vmem(*arrays):
+    return [pltpu.with_memory_space_constraint(array, pltpu.VMEM) for array in arrays]
 
 
 def in_hbm(array):
@@ -586,74 +628,71 @@
         out_shape=(shaped(*layers), shaped(*layers), shaped(8, columns)),
         in_specs=[VMEM] * 4,
         out_specs=(VMEM,) * 3,
-        compiler_params=params(4),
+        compiler_params=params(2),
         cost_estimate=pl.CostEstimate(flops=COST, bytes_accessed=2**20, transcendentals=0),
         name="center_first",
-    )(height, divergence, courant_x, courant_y)
+    )(*in_vmem(height, divergence, courant_x, courant_y))
 
     x_even_out, x_odd_out = pl.pallas_call(
         bind(middle_kernel, rows),
         out_shape=(shaped(MESSAGE, 8, columns),) * 2,
         in_specs=[VMEM] * 9,
         out_specs=(VMEM,) * 2,
-        compiler_params=params(4),
+        compiler_params=params(2),
         name="middle",
-    )(even_in, odd_in, even_out, odd_out, height, divergence, courant_x, courant_y, token)
+    )(*in_vmem(even_in, odd_in, even_out, odd_out, height, divergence, courant_x, courant_y, token))
     x_even_in = lax.ppermute(x_even_out, "gx", pairs("gx", 0))
     x_odd_in = lax.ppermute(x_odd_out, "gx", pairs("gx", 1))
 
-    center = pl.pallas_call(
+    center, _ = pl.pallas_call(
         bind(center_second_kernel, rows, ITERS - ITERS // 2),
-        out_shape=shaped(*layers),
+        out_shape=(shaped(*layers),) * 2,
         in_specs=[VMEM] * 4,
-        out_specs=VMEM,
-        scratch_shapes=[field],
-        compiler_params=params(4),
+        out_specs=(VMEM,) * 2,
+        input_output_aliases={0: 0, 1: 1},
+        compiler_params=params(2),
         cost_estimate=pl.CostEstimate(flops=COST, bytes_accessed=2**20, transcendentals=0),
         name="center_second",
-    )(center_h, center_d, courant_x, courant_y)
+    )(*in_vmem(center_h, center_d, courant_x, courant_y))
 
     count = rows // 2 + W
     packed = (count + 8, gauges, columns)
-    partial_out, bh0, bd0, cbx, cby, sums, homes = pl.pallas_call(
+    merged, bh0, bd0, cbx, cby, sums, homes = pl.pallas_call(
         bind(strips_kernel, rows),
         out_shape=(
-            shaped(*flat), shaped(*packed), shaped(*packed), shaped(count, columns), shaped(count, columns),
+            shaped(rows, gauges, columns), shaped(*packed), shaped(*packed), shaped(count, columns), shaped(count, columns),
             shaped(slots_x, 8, columns), shaped(slots, columns, dtype=jnp.int32),
         ),
         in_specs=[VMEM] * 11 + [SMEM] * 2,
-        out_specs=(HBM,) + (VMEM,) * 6,
-        scratch_shapes=[pltpu.VMEM(packed, F32), pltpu.VMEM(packed, F32), field]
-        + [pltpu.VMEM((vectors, 8, columns), F32)] * 2
-        + [pltpu.SemaphoreType.DMA],
-        compiler_params=params(8),
+        out_specs=(VMEM,) * 7,
+        scratch_shapes=[pltpu.VMEM(packed, F32)] * 2 + [pltpu.VMEM((vectors, 8, columns), F32)] * 2,
+        compiler_params=params(5),
         cost_estimate=pl.CostEstimate(flops=COST, bytes_accessed=2**20, transcendentals=0),
         name="strips",
     )(
-        even_in, odd_in, even_out, odd_out, height, divergence, courant_x, courant_y, center,
-        land_sea, uplift, tile_patches.reshape(-1), patch_home,
+        *in_vmem(even_in, odd_in, even_out, odd_out, height, divergence, courant_x, courant_y, center),
+        land_sea, uplift, tile_patches, patch_home,
     )
 
     depth = 3 * W
     out, message = pl.pallas_call(
         bind(bands_kernel, rows),
         out_shape=(shaped(*flat), shaped(devices, columns)),
-        in_specs=[VMEM] * 14 + [HBM],
+        in_specs=[VMEM] * 15,
         out_specs=(HBM, VMEM),
-        input_output_aliases={14: 0},
         scratch_shapes=[
             pltpu.VMEM((3, depth, 8, columns), F32),
             pltpu.VMEM((3, depth, 8, columns), F32),
             pltpu.VMEM((3, depth, columns), F32),
             pltpu.VMEM((3, depth, columns), F32),
             pltpu.VMEM((2 * W, 8, columns), F32),
-            pltpu.SemaphoreType.DMA,
+            pltpu.SemaphoreType.DMA((24,)),
         ],
-        compiler_params=params(4),
+        compiler_params=params(2),
         name="bands",
     )(
-        x_even_in, x_odd_in, height, divergence, courant_x, courant_y, bh0, bd0, cbx, cby,
-        land_sea, uplift, sums, homes, partial_out,
+        *in_vmem(x_even_in, x_odd_in, height, divergence, courant_x, courant_y, bh0, bd0, cbx, cby),
+        land_sea, uplift, *in_vmem(sums, homes, merged),
     )
     received = lax.all_to_all(message, ("gx", "gy"), 0, 0, tiled=True)
     gradient = pl.pallas_call(
@@ -666,7 +705,7 @@
     return (out.reshape(gauges, rows, columns), gradient)
 
 
-LOAD_MIB = 8
+LOAD_MIB = 6
 COST = 40_000_000
 
 

time: 66.4 us -> 43.6 us (0.66)
  Pallas kernels: 41.4 us -> 20.2 us
  local copies, waits for them, and re-layouts: 1.4 us -> 0.03 us
  starting transfers between devices: 5.04 us -> 4.36 us
    pallas_call x1, Pallas kernels: 27.6 us -> 7.35 us  [body(): pl.pallas_call(bind(strips_kernel, rows), out_shape=(shaped(rows, gauges,...]
    unnamed x28 -> x8, local copies, waits for them, and re-layouts: 1.29 us -> 0.03 us
    pallas_call x1, Pallas kernels: 1.05 us -> 0.16 us  [body(): pl.pallas_call(bind(middle_kernel, rows), out_shape=(shaped(MESSAGE, 8, c...]
  transfers between devices with their start and end apart: 4 -> 4, of which waited for: 0 -> 0; matrix products, arithmetic and copies ran while one was open for 0% -> 0% of each run, Pallas kernels for 49% -> 29%
where the time goes in v2:
time: 43.6 us; the launch traced here: 43.3 us
  Pallas kernels  20.2 us (46%)
  blocking collectives  17.9 us (41%)
  starting transfers between devices  4.36 us (10%)
  between operations  0.77 us (2%)
    all_to_all x1, blocking collectives, body(): received = lax.all_to_all(message, ('gx', 'gy'), 0, 0, tiled=True)  17.9 us
    pallas_call x1, Pallas kernels, body(): pl.pallas_call(bind(strips_kernel, rows), out_shape=(shaped(rows, gauges,...  7.35 us
    pallas_call x1, Pallas kernels, body(): pl.pallas_call(bind(bands_kernel, rows), out_shape=(shaped(*flat), shaped...  3.09 us
    pallas_call x1, Pallas kernels, body(): pl.pallas_call(bind(load_kernel, rows), out_shape=(shaped(*layers), shape...  2.97 us
    pallas_call x1, Pallas kernels, body(): pl.pallas_call(bind(center_second_kernel, rows, ITERS - ITERS // 2), out_...  2.69 us
    pallas_call x1, Pallas kernels, body(): pl.pallas_call(bind(center_first_kernel, rows, ITERS // 2), out_shape=(sh...  2.53 us
    ppermute x1, starting transfers between devices, body(): x_even_in = lax.ppermute(x_even_out, 'gx', pairs('gx', 0))  2.52 us
    pallas_call x1, Pallas kernels, body(): pl.pallas_call(final_kernel, out_shape=shaped(patch_home.shape[0] // devi...  1.39 us
  transfers between devices with their start and end apart: 4, of which 0 were waited for; matrix products, arithmetic and copies ran while one was open for 0% of the time, Pallas kernels for 29%

profile of v2, /device:TPU:0, one launch (start us, length us, event | category | flops | bytes accessed | tf_op | source)
XLA Modules:
  0.0 43.3 jit_solution(7630977180022632557)
XLA Ops:
  0.6 3.0 %load.1 = (f32[264,8,128]{2,1,0:T(8,128)S(1)}, f32[264,8,128]{2,1,0:T(8,128)S(1)}, f32[37,8,128]{2,1,0:T(8,128)S(1)}, f32[37,8,128]{2,1,0:T(8,128)S(1)}, f32[256,128]{1,0:T(8,128)S(1)}, /*index=5*/f32[256,128]{1,0:T(8,128)S(1)}) custom-call(f32[2048,128]{1,0:T(8,128)} %bitcast.9, f32[2048,128]{1,0:T(8,128)} %bitcast.10, f32[2048,128]{1,0:T(8,128)} %bitcast.11, ...), custom_call_target="tpu_custom_call" | custom-call | tf_op jit(solution)/shard_map/load/pallas_call | solution.py:604
  3.6 0.5 %collective-permute-start = (f32[37,8,128]{2,1,0:T(8,128)S(1)}, f32[37,8,128]{2,1,0:T(8,128)S(1)}, u32[]{:S(2)}, u32[]{:S(2)}) collective-permute-start(f32[37,8,128]{2,1,0:T(8,128)S(1)} %get-tuple-element.23.refs_2_), channel_id=1, source_target_pairs={{0,1},{1,0},{2,3},{3,2},{4,5},{5,4},{6,7},{7,6},{8,9},{9,8},{10,11... | collective-permute-start | bytes 454664 | tf_op jit(solution)/shard_map/ppermute | solution.py:623
  4.1 0.7 %collective-permute-start.1 = (f32[37,8,128]{2,1,0:T(8,128)S(1)}, f32[37,8,128]{2,1,0:T(8,128)S(1)}, u32[]{:S(2)}, u32[]{:S(2)}) collective-permute-start(f32[37,8,128]{2,1,0:T(8,128)S(1)} %get-tuple-element.24.refs_3_), channel_id=1, source_target_pairs={{1,2},{2,1},{3,4},{4,3},{5,6},{6,5},{9,10},{10,9},{11,12},{12,11},... | collective-permute-start | bytes 454664 | tf_op jit(solution)/shard_map/ppermute | solution.py:624
  4.8 2.5 %center_first.1 = (f32[264,8,128]{2,1,0:T(8,128)S(1)}, f32[264,8,128]{2,1,0:T(8,128)S(1)}, f32[8,128]{1,0:T(8,128)S(1)}) custom-call(f32[264,8,128]{2,1,0:T(8,128)S(1)} %get-tuple-element.25.refs_0_.refs_4_.refs_2_, f32[264,8,128]{2,1,0:T(8,128)S(1)} %get-tuple-element.26.refs_1_.refs_5_.refs_3_, f32[256,128]{1,0:T(8,128)S(1)} %get-tuple-element.27.refs_2_.refs_6_.refs_4_, ...), custom_call_target="tpu_custom_call" | custom-call | flops 40000000 | bytes 1048576 | tf_op jit(solution)/shard_map/center_first/pallas_call | solution.py:626
  7.3 0.0 collective-permute-done.refs_0_
  7.3 0.0 collective-permute-done.1.refs_1_
  7.4 0.2 middle.1
  7.5 2.5 %collective-permute-start.2 = (f32[22,8,128]{2,1,0:T(8,128)S(1)}, f32[22,8,128]{2,1,0:T(8,128)S(1)}, u32[]{:S(2)}, u32[]{:S(2)}) collective-permute-start(f32[22,8,128]{2,1,0:T(8,128)S(1)} %get-tuple-element.30), channel_id=1, source_target_pairs={{0,8},{8,0},{16,24},{24,16},{1,9},{9,1},{17,25},{25,17},{2,10},{10... | collective-permute-start | bytes 270344 | tf_op jit(solution)/shard_map/ppermute | solution.py:644
  10.0 0.7 %collective-permute-start.3 = (f32[22,8,128]{2,1,0:T(8,128)S(1)}, f32[22,8,128]{2,1,0:T(8,128)S(1)}, u32[]{:S(2)}, u32[]{:S(2)}) collective-permute-start(f32[22,8,128]{2,1,0:T(8,128)S(1)} %get-tuple-element.31), channel_id=1, source_target_pairs={{8,16},{16,8},{9,17},{17,9},{10,18},{18,10},{11,19},{19,11},{12,20... | collective-permute-start | bytes 270344 | tf_op jit(solution)/shard_map/ppermute | solution.py:645
  10.7 0.0 copy-start
  10.7 0.0 copy-start.1
  10.7 0.0 copy-start.2
  10.7 0.0 copy-start.3
  10.8 2.7 %center_second.1 = (f32[264,8,128]{2,1,0:T(8,128)S(1)}, f32[264,8,128]{2,1,0:T(8,128)S(1)}) custom-call(f32[264,8,128]{2,1,0:T(8,128)S(1)} %get-tuple-element.32.refs_0_, f32[264,8,128]{2,1,0:T(8,128)S(1)} %get-tuple-element.33.refs_1_, f32[256,128]{1,0:T(8,128)S(1)} %get-tuple-element.27.refs_2_.refs_6_.refs_4_, ...), custom_call_target="tpu_custom_call", output_to_operand_aliasing={{0}: (0, {}), {1}: (1, {})} | custom-call | flops 40000000 | bytes 1048576 | tf_op jit(solution)/shard_map/center_second/pallas_call | solution.py:647
  13.4 0.0 copy-done
  13.4 0.0 copy-done.1
  13.5 0.0 copy-done.2
  13.5 0.0 copy-done.3
  13.5 7.4 %strips.1 = (f32[256,8,128]{2,1,0:T(8,128)S(1)}, f32[144,8,128]{2,1,0:T(8,128)S(1)}, f32[144,8,128]{2,1,0:T(8,128)S(1)}, f32[136,128]{1,0:T(8,128)S(1)}, f32[136...) custom-call(f32[37,8,128]{2,1,0:T(8,128)S(1)} %collective-permute-done.refs_0_, ...), custom_call_target="tpu_custom_call" | custom-call | flops 40000000 | bytes 1048576 | tf_op jit(solution)/shard_map/strips/pallas_call | solution.py:660
  20.8 0.0 collective-permute-done.2.refs_0_
  20.9 0.0 collective-permute-done.3.refs_1_
  20.9 3.1 %bands.1 = (f32[2048,128]{1,0:T(8,128)}, f32[32,128]{1,0:T(8,128)S(1)}) custom-call(f32[22,8,128]{2,1,0:T(8,128)S(1)} %collective-permute-done.2.refs_0_, f32[22,8,128]{2,1,0:T(8,128)S(1)} %collective-permute-done.3.refs_1_, f32[264,8,128]{2,1,0:T(8,128)S(1)} %get-tuple-element.25.refs_0_.refs_4_.refs_2_, ...), custom_call_target="tpu_custom_call" | custom-call | tf_op jit(solution)/shard_map/bands/pallas_call | solution.py:678
  24.0 17.9 %all_to_all.11 = f32[32,1,128]{2,1,0:T(1,128)} all-to-all(f32[32,1,128]{2,1,0:T(1,128)S(1)} %bitcast.8), channel_id=1, replica_groups=mesh['gx'=4,'gy'=8] {'gx','gy'}, dimensions={0} | all-to-all | bytes 32768 | tf_op jit(solution)/shard_map/all_to_all | solution.py:697
  41.9 1.4 %final.1 = f32[8,8]{1,0:T(8,128)} custom-call(f32[32,128]{1,0:T(8,128)} %bitcast.12), custom_call_target="tpu_custom_call" | custom-call | tf_op jit(solution)/shard_map/final/pallas_call | solution.py:698
Async XLA Ops:
  3.6 3.7 %collective-permute-start = (f32[37,8,128]{2,1,0:T(8,128)S(1)}, f32[37,8,128]{2,1,0:T(8,128)S(1)}, u32[]{:S(2)}, u32[]{:S(2)}) collective-permute-start(f32[37,8,128]{2,1,0:T(8,128)S(1)} %get-tuple-element.23.refs_2_), channel_id=1, source_target_pairs={{0,1},{1,0},{2,3},{3,2},{4,5},{5,4},{6,7},{7,6},{8,9},{9,8},{10,11... | collective-permute-start | bytes 454664 | tf_op jit(solution)/shard_map/ppermute | solution.py:623
  4.1 3.2 %collective-permute-start.1 = (f32[37,8,128]{2,1,0:T(8,128)S(1)}, f32[37,8,128]{2,1,0:T(8,128)S(1)}, u32[]{:S(2)}, u32[]{:S(2)}) collective-permute-start(f32[37,8,128]{2,1,0:T(8,128)S(1)} %get-tuple-element.24.refs_3_), channel_id=1, source_target_pairs={{1,2},{2,1},{3,4},{4,3},{5,6},{6,5},{9,10},{10,9},{11,12},{12,11},... | collective-permute-start | bytes 454664 | tf_op jit(solution)/shard_map/ppermute | solution.py:624
  7.5 13.3 %collective-permute-start.2 = (f32[22,8,128]{2,1,0:T(8,128)S(1)}, f32[22,8,128]{2,1,0:T(8,128)S(1)}, u32[]{:S(2)}, u32[]{:S(2)}) collective-permute-start(f32[22,8,128]{2,1,0:T(8,128)S(1)} %get-tuple-element.30), channel_id=1, source_target_pairs={{0,8},{8,0},{16,24},{24,16},{1,9},{9,1},{17,25},{25,17},{2,10},{10... | collective-permute-start | bytes 270344 | tf_op jit(solution)/shard_map/ppermute | solution.py:644
  10.0 10.8 %collective-permute-start.3 = (f32[22,8,128]{2,1,0:T(8,128)S(1)}, f32[22,8,128]{2,1,0:T(8,128)S(1)}, u32[]{:S(2)}, u32[]{:S(2)}) collective-permute-start(f32[22,8,128]{2,1,0:T(8,128)S(1)} %get-tuple-element.31), channel_id=1, source_target_pairs={{8,16},{16,8},{9,17},{17,9},{10,18},{18,10},{11,19},{19,11},{12,20... | collective-permute-start | bytes 270344 | tf_op jit(solution)/shard_map/ppermute | solution.py:645
  10.7 2.7 %copy-start = (s32[256,128]{1,0:T(8,128)S(1)}, s32[256,128]{1,0:T(8,128)}, u32[]{:S(2)}) copy-start(s32[256,128]{1,0:T(8,128)} %refs_10_.3) | copy-start | bytes 393220
  10.7 2.7 %copy-start.1 = (f32[256,128]{1,0:T(8,128)S(1)}, f32[256,128]{1,0:T(8,128)}, u32[]{:S(2)}) copy-start(f32[256,128]{1,0:T(8,128)} %refs_11_.3) | copy-start | bytes 393220
  10.7 2.7 %copy-start.2 = (s32[4,8,15]{2,1,0:T(8,128)S(1)}, s32[4,8,15]{2,1,0:T(8,128)}, u32[]{:S(2)}) copy-start(s32[4,8,15]{2,1,0:T(8,128)} %refs_11_.2) | copy-start | bytes 5764
  10.7 2.7 %copy-start.3 = (s32[256]{0:T(256)S(1)}, s32[256]{0:T(256)}, u32[]{:S(2)}) copy-start(s32[256]{0:T(256)} %refs_12_.1) | copy-start | bytes 3076

commit v3 on v2

--- a/solution.py
+++ b/solution.py
@@ -12,7 +12,6 @@
 GROUPS = LANES // W
 F32 = jnp.float32
 VMEM = pl.BlockSpec(memory_space=pltpu.VMEM)
-SMEM = pl.BlockSpec(memory_space=pltpu.SMEM)
 HBM = pl.BlockSpec(memory_space=pl.ANY)
 
 
@@ -94,31 +93,18 @@
         self.waiting = self.waiting[count:] if count else []
 
 
-def rows_of(count, refs):
-    return [refs + (r, False, "item" if r + 1 < count else None) for r in range(count)]
-
-
-def run_steps(count, steps, unroll, first, then, lag):
-    if first is not None:
-        head = rows_of(count, first)
-        for _ in range(unroll - 1):
-            head = head + rows_of(count, then)
-        advance(head, lag)
-
-    def again(t, carry):
-        advance(rows_of(count, then) * unroll, lag)
-        return carry
-
-    rounds = steps // unroll - (first is not None)
-    if rounds == 1:
-        again(0, 0)
-    elif rounds:
-        lax.fori_loop(0, rounds, again, 0)
+def run_steps(count, steps, first, then, lag):
+    items = []
+    for t in steps:
+        refs = first if t == steps[0] else then
+        for r in range(t, count - t):
+            items.append(refs + (r, t > 0, "item" if r + 1 < count - t else "row" if t else None))
+    advance(items, lag)
 
 
 def load_kernel(
-    rows, h_hbm, x_hbm, y_hbm, cx_hbm, cy_hbm, wet_hbm,
-    h_out, d_out, even_out, odd_out, cx_ref, cy_ref, hb, xb, yb, wet_ref, sems,
+    rows, h_hbm, x_hbm, y_hbm, cx_hbm, cy_hbm, wet_hbm, lists_hbm, home_hbm,
+    h_out, d_out, odd_out, even_out, cx_ref, cy_ref, homes, hb, xb, yb, wet_ref, lists_ref, home_ref, sems,
 ):
     gauges = 8
     parts = 4
@@ -127,7 +113,11 @@
         pltpu.make_async_copy(source, target, sems.at[parts + i])
         for i, (source, target) in enumerate(((cx_hbm, cx_ref), (cy_hbm, cy_ref), (wet_hbm, wet_ref)))
     ]
-    for copy in plain:
+    scalars = [
+        pltpu.make_async_copy(lists_hbm, lists_ref, sems.at[parts + 3]),
+        pltpu.make_async_copy(home_hbm, home_ref, sems.at[parts + 4]),
+    ]
+    for copy in plain + scalars:
         copy.start()
     for part in range(parts):
         for source, target in ((y_hbm, yb), (x_hbm, xb), (h_hbm, hb)):
@@ -201,17 +191,24 @@
     d_out[rows] = -above
     put(at_g, -above, roll(-above, W))
 
+    for copy in scalars:
+        copy.wait()
+    tile_row, tile_column = lax.axis_index("gx"), lax.axis_index("gy")
+    for slot in range(homes.shape[0]):
+        patch = lists_ref[tile_row, tile_column, slot]
+        homes[pl.ds(slot, 1), :] = jnp.full((1, LANES), home_ref[patch], jnp.int32)
+
 
 def center_first_kernel(rows, steps, h_ref, d_ref, cx_ref, cy_ref, h_out, d_out, token):
     first = (h_ref, d_ref, h_out, d_out, cx_ref, cy_ref)
     then = (h_out, d_out, h_out, d_out, cx_ref, cy_ref)
-    run_steps(rows, steps, 2, first, then, 24)
+    run_steps(rows, steps, first, then, 32)
     token[...] = jnp.zeros((8, LANES), F32)
 
 
 def center_second_kernel(rows, steps, h_in, d_in, cx_ref, cy_ref, h_out, d_out):
     then = (h_out, d_out, h_out, d_out, cx_ref, cy_ref)
-    run_steps(rows, steps, 2, None, then, 24)
+    run_steps(rows, steps, then, then, 32)
 
 
 SECOND = 32
@@ -317,8 +314,8 @@
 
 
 def strips_kernel(
-    rows, even_in, odd_in, even_out, odd_out, h_ref, d_ref, cx_ref, cy_ref, done_ref, wet_ref, uplift_ref, lists_ref, home_ref,
-    merged, bh0, bd0, cbx, cby, sums, homes, hb, db, lefts, rights,
+    rows, even_in, odd_in, even_out, odd_out, h_ref, d_ref, cx_ref, cy_ref, done_ref, wet_ref, uplift_ref,
+    merged, bh0, bd0, cbx, cby, sums, hb, db, lefts, rights,
 ):
     side = Sides(even_in, odd_in, even_out, odd_out)
     lane = side.lane
@@ -354,25 +351,21 @@
         return height, strip_divergence(lane, d_ref[row], left, right, shift)
 
     def build(b, length):
-        values = []
         for k in range(length):
             row = b * GROUPS + k
             upper = strips_at(row, b, k, 0)
             lower_m, lower_k = divmod(offset + k, GROUPS)
             lower = strips_at(row + offset, b + lower_m, lower_k, SECOND)
-            values.append([jnp.where(second, low, up) for up, low in zip(upper, lower)])
-        for k in range(length):
-            bh0[b * GROUPS + k], bd0[b * GROUPS + k] = values[k]
-        return length
-
-    lax.fori_loop(0, count // GROUPS, lambda b, carry: build(b, GROUPS) and carry, 0)
-    if count % GROUPS:
-        build(count // GROUPS, count % GROUPS)
+            store(bh0, row, jnp.where(second, lower[0], upper[0]))
+            store(bd0, row, jnp.where(second, lower[1], upper[1]))
+
+    for b in range(0, count, GROUPS):
+        build(b // GROUPS, min(GROUPS, count - b))
     store.release()
     bd0[count] = strip(lane, d_ref[rows], roll(lefts[at_g], 64 - W), rights[at_g])
     first = (bh0, bd0, hb, db, cbx, cby)
     then = (hb, db, hb, db, cbx, cby)
-    run_steps(count, ITERS, 2, first, then, 24)
+    run_steps(count, range(ITERS), first, then, 24)
 
     bounds = slot_bounds(rows)
     for u in range(len(bounds) - 1):
@@ -385,11 +378,6 @@
             total = total + weight * value
         store(sums, u, total)
     store.release()
-    tile_row, tile_column = lax.axis_index("gx"), lax.axis_index("gy")
-    slots = homes.shape[0]
-    for s in range(slots):
-        patch = lists_ref[tile_row, tile_column, s]
-        homes[pl.ds(s, 1), :] = jnp.full((1, LANES), home_ref[patch], jnp.int32)
 
 
 def slot_bounds(length):
@@ -397,18 +385,9 @@
 
 
 def bands_kernel(
-    rows, x_even_in, x_odd_in, h_ref, d_ref, cx_ref, cy_ref, bh0, bd0, cbx, cby, done_wet, uplift_ref, sums_ref, homes_ref, merged,
-    out_hbm, message, hs, ds, cxs, cys, edge, sems,
+    rows, x_even_in, x_odd_in, h_ref, d_ref, cx_ref, cy_ref, bh0, bd0, cbx, cby, done_wet, uplift_ref, sums_ref, homes_ref,
+    edge, message, hs, ds, cxs, cys,
 ):
-    inner = rows - 2 * W
-    copies = [
-        pltpu.make_async_copy(
-            merged.at[pl.ds(W, inner), g], out_hbm.at[pl.ds(g * rows + W, inner)], sems.at[g]
-        )
-        for g in range(8)
-    ]
-    for copy in copies:
-        copy.start()
     lane = lanes_of()
     second = second_lanes(lane)
     even = lax.rem(lax.axis_index("gx"), 2) == 0
@@ -429,16 +408,11 @@
     top, bottom, strips = 0, 1, 2
     for c, (ref, mine, packed) in enumerate(((cxs, cx_ref, cbx), (cys, cy_ref, cby))):
         halos = []
-        for got in (above, below):
+        for got, shift in ((above, 0), (below, SECOND)):
             value, corner = got(2 * W + 2 + c), got(2 * W + 4)
-            halos.append(
-                (
-                    value,
-                    strip(
-                        lane, value, roll(corner, 64 - W - 2 * W * c), roll(corner, -W - 2 * W * c)
-                    ),
-                )
-            )
+            left = roll(corner, 64 - W - 2 * W * c + shift)
+            right = roll(corner, shift - W - 2 * W * c)
+            halos.append((value, strip(lane, value, left, right, shift)))
         store(ref, (top, slice(0, W)), halos[0][0])
         store(ref, (top, slice(W, depth)), mine[0 : 2 * W, :])
         store(ref, (bottom, slice(0, 2 * W)), mine[rows - 2 * W : rows, :])
@@ -446,23 +420,20 @@
         store(ref, (strips, slice(0, W)), both(halos[0][1], packed[count - 2 * W : count - W, :]))
         store(ref, (strips, slice(W, 2 * W)), both(packed[0:W, :], packed[count - W : count, :]))
         store(
-            ref, (strips, slice(2 * W, depth)), both(packed[W : 2 * W, :], roll(halos[1][1], SECOND))
+            ref, (strips, slice(2 * W, depth)), both(packed[W : 2 * W, :], halos[1][1])
         )
 
-    def halo_strips(got, j):
+    def halo_strips(got, j, shift):
         packed_h, packed_d = got(2 * W), got(2 * W + 1)
-        return (
-            strip(lane, got(j), roll(packed_h, 64 - W - W * j), roll(packed_h, -64 - W * j)),
-            strip_divergence(
-                lane, got(W + j), roll(packed_d, 64 - W + 1 - W * j), roll(packed_d, -64 - W * j)
-            ),
-        )
+        left, right = roll(packed_h, 64 - W - W * j + shift), roll(packed_h, shift - 64 - W * j)
+        height = strip(lane, got(j), left, right, shift)
+        left, right = roll(packed_d, 64 - W + 1 - W * j + shift), roll(packed_d, shift - 64 - W * j)
+        return height, strip_divergence(lane, got(W + j), left, right, shift)
 
     flux, corner = above(2 * W + 5), above(2 * W + 4)
     flux_strip = strip(lane, flux, roll(corner, 64 - W - 4 * W), roll(corner, -5 * W))
     for j in range(W):
-        upper, lower = halo_strips(above, j), halo_strips(below, j)
-        h_last, d_last = roll(lower[0], SECOND), roll(lower[1], SECOND)
+        upper, (h_last, d_last) = halo_strips(above, j, 0), halo_strips(below, j, SECOND)
         d_first, d_below = bd0[j], below(W + j)
         d_top = d_ref[j]
         if j == 0:
@@ -506,18 +477,6 @@
             weight = done_wet[pl.ds(first + j, 1), :].astype(F32) * uplift_ref[pl.ds(first + j, 1), :] * (1.0 / BS)
             totals[slot] = totals[slot] + weight * value
     store.release()
-    edges = [
-        pltpu.make_async_copy(
-            edge.at[pl.ds(band * W, W), g],
-            out_hbm.at[pl.ds(g * rows + first, W)],
-            sems.at[8 + 8 * band + g],
-        )
-        for band, first in ((0, 0), (1, rows - W))
-        for g in range(8)
-    ]
-    for copy in edges:
-        copy.start()
-
     column_bounds = slot_bounds(LANES)
     slots_y = len(column_bounds) - 1
     devices = message.shape[0]
@@ -539,18 +498,28 @@
             home = homes_ref[pl.ds(u * slots_y + w, 1), :]
             built = built + jnp.where(home_of == home, spread, 0.0)
     message[...] = built
-    for copy in copies + edges:
+
+
+def write_kernel(rows, merged, edge, out_hbm, sems):
+    inner = rows - 2 * W
+    copies = []
+    for g in range(8):
+        for source, at, first, length in (
+            (merged, W, W, inner),
+            (edge, 0, 0, W),
+            (edge, W, rows - W, W),
+        ):
+            copies.append(
+                pltpu.make_async_copy(
+                    source.at[pl.ds(at, length), g],
+                    out_hbm.at[pl.ds(g * rows + first, length)],
+                    sems.at[len(copies)],
+                )
+            )
+    for copy in copies:
+        copy.start()
+    for copy in copies:
         copy.wait()
-
-
-def final_kernel(received, gradient):
-    total = jnp.sum(received[...], axis=0, keepdims=True)
-    lane = lanes_of()
-    row = lax.broadcasted_iota(jnp.int32, (8, LANES), 0)
-    result = jnp.zeros((8, LANES), F32)
-    for k in range(8):
-        result = jnp.where(row == k, roll(jnp.broadcast_to(total, (8, LANES)), -8 * k), result)
-    gradient[...] = result[:, :8]
 
 
 def pairs(axis, first):
@@ -601,15 +570,21 @@
     field = pltpu.VMEM((rows, gauges, columns), F32)
     work = pltpu.VMEM(layers, F32)
 
-    height, divergence, even_out, odd_out, courant_x, courant_y = pl.pallas_call(
+    height, divergence, odd_out, even_out, courant_x, courant_y, homes = pl.pallas_call(
         bind(load_kernel, rows),
         out_shape=(
             shaped(*layers), shaped(*layers), shaped(vectors, 8, columns), shaped(vectors, 8, columns),
-            shaped(rows, columns), shaped(rows, columns),
+            shaped(rows, columns), shaped(rows, columns), shaped(slots, columns, dtype=jnp.int32),
         ),
-        in_specs=[HBM] * 6,
-        out_specs=(VMEM,) * 6,
-        scratch_shapes=[field] * 3 + [pltpu.VMEM((rows, columns), jnp.int32), pltpu.SemaphoreType.DMA((7,))],
+        in_specs=[HBM] * 8,
+        out_specs=(VMEM,) * 7,
+        scratch_shapes=[field] * 3
+        + [
+            pltpu.VMEM((rows, columns), jnp.int32),
+            pltpu.SMEM(tile_patches.shape, jnp.int32),
+            pltpu.SMEM(patch_home.shape, jnp.int32),
+            pltpu.SemaphoreType.DMA((9,)),
+        ],
         compiler_params=params(LOAD_MIB),
         name="load",
     )(
@@ -619,12 +594,14 @@
         in_hbm(courant_x),
         in_hbm(courant_y),
         in_hbm(land_sea),
-    )
+        in_hbm(tile_patches),
+        in_hbm(patch_home),
+    )
+    odd_in = lax.ppermute(odd_out, "gy", pairs("gy", 1))
     even_in = lax.ppermute(even_out, "gy", pairs("gy", 0))
-    odd_in = lax.ppermute(odd_out, "gy", pairs("gy", 1))
 
     center_h, center_d, token = pl.pallas_call(
-        bind(center_first_kernel, rows, ITERS // 2),
+        bind(center_first_kernel, rows, range(EARLY)),
         out_shape=(shaped(*layers), shaped(*layers), shaped(8, columns)),
         in_specs=[VMEM] * 4,
         out_specs=(VMEM,) * 3,
@@ -645,7 +622,7 @@
     x_odd_in = lax.ppermute(x_odd_out, "gx", pairs("gx", 1))
 
     center, _ = pl.pallas_call(
-        bind(center_second_kernel, rows, ITERS - ITERS // 2),
+        bind(center_second_kernel, rows, range(EARLY, ITERS)),
         out_shape=(shaped(*layers),) * 2,
         in_specs=[VMEM] * 4,
         out_specs=(VMEM,) * 2,
@@ -657,56 +634,59 @@
 
     count = rows // 2 + W
     packed = (count + 8, gauges, columns)
-    merged, bh0, bd0, cbx, cby, sums, homes = pl.pallas_call(
+    merged, bh0, bd0, cbx, cby, sums = pl.pallas_call(
         bind(strips_kernel, rows),
         out_shape=(
             shaped(rows, gauges, columns), shaped(*packed), shaped(*packed), shaped(count, columns), shaped(count, columns),
-            shaped(slots_x, 8, columns), shaped(slots, columns, dtype=jnp.int32),
+            shaped(slots_x, 8, columns),
         ),
-        in_specs=[VMEM] * 11 + [SMEM] * 2,
-        out_specs=(VMEM,) * 7,
+        in_specs=[VMEM] * 11,
+        out_specs=(VMEM,) * 6,
         scratch_shapes=[pltpu.VMEM(packed, F32)] * 2 + [pltpu.VMEM((vectors, 8, columns), F32)] * 2,
         compiler_params=params(5),
         cost_estimate=pl.CostEstimate(flops=COST, bytes_accessed=2**20, transcendentals=0),
         name="strips",
     )(
         *in_vmem(even_in, odd_in, even_out, odd_out, height, divergence, courant_x, courant_y, center),
-        land_sea, uplift, tile_patches, patch_home,
+        land_sea, uplift,
     )
 
     depth = 3 * W
-    out, message = pl.pallas_call(
+    edge, message = pl.pallas_call(
         bind(bands_kernel, rows),
-        out_shape=(shaped(*flat), shaped(devices, columns)),
-        in_specs=[VMEM] * 15,
-        out_specs=(HBM, VMEM),
+        out_shape=(shaped(2 * W, gauges, columns), shaped(devices, columns)),
+        in_specs=[VMEM] * 14,
+        out_specs=(VMEM,) * 2,
         scratch_shapes=[
             pltpu.VMEM((3, depth, 8, columns), F32),
             pltpu.VMEM((3, depth, 8, columns), F32),
             pltpu.VMEM((3, depth, columns), F32),
             pltpu.VMEM((3, depth, columns), F32),
-            pltpu.VMEM((2 * W, 8, columns), F32),
-            pltpu.SemaphoreType.DMA((24,)),
         ],
         compiler_params=params(2),
         name="bands",
     )(
         *in_vmem(x_even_in, x_odd_in, height, divergence, courant_x, courant_y, bh0, bd0, cbx, cby),
-        land_sea, uplift, *in_vmem(sums, homes, merged),
+        land_sea, uplift, *in_vmem(sums, homes),
     )
     received = lax.all_to_all(message, ("gx", "gy"), 0, 0, tiled=True)
-    gradient = pl.pallas_call(
-        final_kernel,
-        out_shape=shaped(patch_home.shape[0] // devices, gauges),
-        in_specs=[VMEM],
-        out_specs=VMEM,
-        name="final",
-    )(received)
+    out = pl.pallas_call(
+        bind(write_kernel, rows),
+        out_shape=shaped(*flat),
+        in_specs=[VMEM] * 2,
+        out_specs=HBM,
+        scratch_shapes=[pltpu.SemaphoreType.DMA((24,))],
+        compiler_params=params(1),
+        name="write",
+    )(*in_vmem(merged, edge))
+    per_device = patch_home.shape[0] // devices
+    gradient = jnp.sum(received, axis=0)[: per_device * gauges].reshape(per_device, gauges)
     return (out.reshape(gauges, rows, columns), gradient)
 
 
 LOAD_MIB = 6
 COST = 40_000_000
+EARLY = 5
 
 
 def solution(mesh):

time: 43.6 us -> 39.8 us (0.913)
  blocking collectives: 17.9 us -> 0 us
  starting transfers between devices: 4.36 us -> 14.6 us
  waiting for transfers between devices: 0.01 us -> 5.94 us
  Pallas kernels: 20.2 us -> 17.6 us
  local copies, waits for them, and re-layouts: 0.03 us -> 0.69 us
    all_to_all x1 -> x0, blocking collectives: 17.9 us -> none  [body(): received = lax.all_to_all(message, ('gx', 'gy'), 0, 0, tiled=True)]
    all_to_all x0 -> x1, starting transfers between devices: none -> 10 us  [body(): received = lax.all_to_all(message, ('gx', 'gy'), 0, 0, tiled=True)]
    all_to_all x0 -> x1, waiting for transfers between devices: none -> 5.93 us  [body(): received = lax.all_to_all(message, ('gx', 'gy'), 0, 0, tiled=True)]
    pallas_call x1, Pallas kernels: 7.35 us -> 5.23 us  [body(): pl.pallas_call(bind(strips_kernel, rows), out_shape=(shaped(rows, gauges,...]
    reshape x0 -> x1, local copies, waits for them, and re-layouts: none -> 0.68 us  [body(): jnp.sum(received, axis=0)[:per_device * gauges].reshape(per_device, gauges)]
    pallas_call x4, Pallas kernels: 9.71 us -> 9.15 us  [the longest x1 3.39 us: body(): pl.pallas_call(bind(center_first_kernel, rows, range(EARLY)), out_shape=(...]
  transfers between devices with their start and end apart: 4 -> 5, of which waited for: 0 -> 1; matrix products, arithmetic and copies ran while one was open for 0% -> 0% of each run, Pallas kernels for 29% -> 30%
where the time goes in v3:
time: 39.8 us; the launch traced here: 39.6 us
  Pallas kernels  17.6 us (44%)
  starting transfers between devices  14.6 us (37%)
  waiting for transfers between devices  5.94 us (15%)
  between operations  0.75 us (2%)
  local copies, waits for them, and re-layouts  0.69 us (2%)
    all_to_all x1, starting transfers between devices, body(): received = lax.all_to_all(message, ('gx', 'gy'), 0, 0, tiled=True)  10 us
    all_to_all x1, waiting for transfers between devices, body(): received = lax.all_to_all(message, ('gx', 'gy'), 0, 0, tiled=True)  5.93 us
    pallas_call x1, Pallas kernels, body(): pl.pallas_call(bind(strips_kernel, rows), out_shape=(shaped(rows, gauges,...  5.23 us
    pallas_call x1, Pallas kernels, body(): pl.pallas_call(bind(center_first_kernel, rows, range(EARLY)), out_shape=(...  3.39 us
    pallas_call x1, Pallas kernels, body(): pl.pallas_call(bind(load_kernel, rows), out_shape=(shaped(*layers), shape...  3.04 us
    pallas_call x1, Pallas kernels, body(): pl.pallas_call(bind(bands_kernel, rows), out_shape=(shaped(2 * W, gauges,...  2.54 us
    ppermute x1, starting transfers between devices, body(): x_even_in = lax.ppermute(x_even_out, 'gx', pairs('gx', 0))  2.52 us
    pallas_call x1, Pallas kernels, body(): pl.pallas_call(bind(center_second_kernel, rows, range(EARLY, ITERS)), out...  2.02 us
  transfers between devices with their start and end apart: 5, of which 1 were waited for; matrix products, arithmetic and copies ran while one was open for 0% of the time, Pallas kernels for 30%

profile of v3, /device:TPU:0, one launch (start us, length us, event | category | flops | bytes accessed | tf_op | source)
XLA Modules:
  0.0 39.6 jit_solution(10609515469656142636)
XLA Ops:
  0.6 3.0 %load.1 = (f32[264,8,128]{2,1,0:T(8,128)S(1)}, f32[264,8,128]{2,1,0:T(8,128)S(1)}, f32[37,8,128]{2,1,0:T(8,128)S(1)}, f32[37,8,128]{2,1,0:T(8,128)S(1)}, f32[256...) custom-call(f32[2048,128]{1,0:T(8,128)} %bitcast.9, f32[2048,128]{1,0:T(8,128)} %bitcast.10, ...), custom_call_target="tpu_custom_call" | custom-call | tf_op jit(solution)/shard_map/load/pallas_call | solution.py:573
  3.7 0.5 %collective-permute-start = (f32[37,8,128]{2,1,0:T(8,128)S(1)}, f32[37,8,128]{2,1,0:T(8,128)S(1)}, u32[]{:S(2)}, u32[]{:S(2)}) collective-permute-start(f32[37,8,128]{2,1,0:T(8,128)S(1)} %get-tuple-element.23.refs_2_), channel_id=1, source_target_pairs={{0,1},{1,0},{2,3},{3,2},{4,5},{5,4},{6,7},{7,6},{8,9},{9,8},{10,11... | collective-permute-start | bytes 454664 | tf_op jit(solution)/shard_map/ppermute | solution.py:601
  4.2 0.7 %collective-permute-start.1 = (f32[37,8,128]{2,1,0:T(8,128)S(1)}, f32[37,8,128]{2,1,0:T(8,128)S(1)}, u32[]{:S(2)}, u32[]{:S(2)}) collective-permute-start(f32[37,8,128]{2,1,0:T(8,128)S(1)} %get-tuple-element.24.refs_3_), channel_id=1, source_target_pairs={{1,2},{2,1},{3,4},{4,3},{5,6},{6,5},{9,10},{10,9},{11,12},{12,11},... | collective-permute-start | bytes 454664 | tf_op jit(solution)/shard_map/ppermute | solution.py:600
  4.9 3.4 %center_first.1 = (f32[264,8,128]{2,1,0:T(8,128)S(1)}, f32[264,8,128]{2,1,0:T(8,128)S(1)}, f32[8,128]{1,0:T(8,128)S(1)}) custom-call(f32[264,8,128]{2,1,0:T(8,128)S(1)} %get-tuple-element.25.refs_0_.refs_4_.refs_2_, f32[264,8,128]{2,1,0:T(8,128)S(1)} %get-tuple-element.26.refs_1_.refs_5_.refs_3_, f32[256,128]{1,0:T(8,128)S(1)} %get-tuple-element.27.refs_2_.refs_6_.refs_4_, ...), custom_call_target="tpu_custom_call" | custom-call | flops 40000000 | bytes 1048576 | tf_op jit(solution)/shard_map/center_first/pallas_call | solution.py:603
  8.3 0.0 collective-permute-done.refs_0_
  8.3 0.0 collective-permute-done.1.refs_1_
  8.3 0.2 middle.1
  8.4 2.5 %collective-permute-start.2 = (f32[22,8,128]{2,1,0:T(8,128)S(1)}, f32[22,8,128]{2,1,0:T(8,128)S(1)}, u32[]{:S(2)}, u32[]{:S(2)}) collective-permute-start(f32[22,8,128]{2,1,0:T(8,128)S(1)} %get-tuple-element.34), channel_id=1, source_target_pairs={{0,8},{8,0},{16,24},{24,16},{1,9},{9,1},{17,25},{25,17},{2,10},{10... | collective-permute-start | bytes 270344 | tf_op jit(solution)/shard_map/ppermute | solution.py:621
  11.0 0.8 %collective-permute-start.3 = (f32[22,8,128]{2,1,0:T(8,128)S(1)}, f32[22,8,128]{2,1,0:T(8,128)S(1)}, u32[]{:S(2)}, u32[]{:S(2)}) collective-permute-start(f32[22,8,128]{2,1,0:T(8,128)S(1)} %get-tuple-element.35), channel_id=1, source_target_pairs={{8,16},{16,8},{9,17},{17,9},{10,18},{18,10},{11,19},{19,11},{12,20... | collective-permute-start | bytes 270344 | tf_op jit(solution)/shard_map/ppermute | solution.py:622
  11.8 0.0 copy-start
  11.8 0.0 copy-start.1
  11.8 2.0 %center_second.1 = (f32[264,8,128]{2,1,0:T(8,128)S(1)}, f32[264,8,128]{2,1,0:T(8,128)S(1)}) custom-call(f32[264,8,128]{2,1,0:T(8,128)S(1)} %get-tuple-element.29.refs_0_, f32[264,8,128]{2,1,0:T(8,128)S(1)} %get-tuple-element.30.refs_1_, f32[256,128]{1,0:T(8,128)S(1)} %get-tuple-element.27.refs_2_.refs_6_.refs_4_, ...), custom_call_target="tpu_custom_call", output_to_operand_aliasing={{0}: (0, {}), {1}: (1, {})} | custom-call | flops 40000000 | bytes 1048576 | tf_op jit(solution)/shard_map/center_second/pallas_call | solution.py:624
  13.9 0.0 copy-done
  13.9 0.0 copy-done.1
  13.9 5.2 %strips.1 = (f32[256,8,128]{2,1,0:T(8,128)S(1)}, f32[144,8,128]{2,1,0:T(8,128)S(1)}, f32[144,8,128]{2,1,0:T(8,128)S(1)}, f32[136,128]{1,0:T(8,128)S(1)}, f32[136...) custom-call(f32[37,8,128]{2,1,0:T(8,128)S(1)} %collective-permute-done.refs_0_, ...), custom_call_target="tpu_custom_call" | custom-call | flops 40000000 | bytes 1048576 | tf_op jit(solution)/shard_map/strips/pallas_call | solution.py:637
  19.1 0.0 collective-permute-done.2.refs_0_
  19.1 0.0 collective-permute-done.3.refs_1_
  19.1 2.5 %bands.1 = (f32[16,8,128]{2,1,0:T(8,128)S(1)}, f32[32,128]{1,0:T(8,128)}) custom-call(f32[22,8,128]{2,1,0:T(8,128)S(1)} %collective-permute-done.2.refs_0_, f32[22,8,128]{2,1,0:T(8,128)S(1)} %collective-permute-done.3.refs_1_, f32[264,8,128]{2,1,0:T(8,128)S(1)} %get-tuple-element.25.refs_0_.refs_4_.refs_2_, ...), custom_call_target="tpu_custom_call" | custom-call | tf_op jit(solution)/shard_map/bands/pallas_call | solution.py:655
  21.7 10.0 %all-to-all-start = ((f32[32,1,128]{2,1,0:T(1,128)}), f32[32,1,128]{2,1,0:T(1,128)S(1)}, u32[]{:S(2)}, u32[]{:S(2)}) async-start(f32[32,1,128]{2,1,0:T(1,128)} %bitcast.5), calls=%async_computation | async-start | bytes 32768 | tf_op jit(solution)/shard_map/all_to_all | solution.py:672
  31.7 1.2 %write.1 = f32[2048,128]{1,0:T(8,128)} custom-call(f32[256,8,128]{2,1,0:T(8,128)S(1)} %get-tuple-element.32.refs_0_, f32[16,8,128]{2,1,0:T(8,128)S(1)} %get-tuple-element.42.refs_1_), custom_call_target="tpu_custom_call" | custom-call | tf_op jit(solution)/shard_map/write/pallas_call | solution.py:673
  32.9 5.9 %all-to-all-done = f32[32,1,128]{2,1,0:T(1,128)S(1)} async-done(((f32[32,1,128]{2,1,0:T(1,128)}), f32[32,1,128]{2,1,0:T(1,128)S(1)}, u32[]{:S(2)}, u32[]{:S(2)}) %all-to-all-start) | async-done | bytes 16416 | tf_op jit(solution)/shard_map/all_to_all | solution.py:672
  38.8 0.1 reduce_sum.9
  38.9 0.7 %reshape.33 = f32[8,8]{1,0:T(8,128)} reshape(f32[64]{0:T(128)S(1)} %bitcast.12) | data formatting | bytes 512 | tf_op jit(solution)/shard_map/reshape | solution.py:683
Async XLA Ops:
  3.7 4.6 %collective-permute-start = (f32[37,8,128]{2,1,0:T(8,128)S(1)}, f32[37,8,128]{2,1,0:T(8,128)S(1)}, u32[]{:S(2)}, u32[]{:S(2)}) collective-permute-start(f32[37,8,128]{2,1,0:T(8,128)S(1)} %get-tuple-element.23.refs_2_), channel_id=1, source_target_pairs={{0,1},{1,0},{2,3},{3,2},{4,5},{5,4},{6,7},{7,6},{8,9},{9,8},{10,11... | collective-permute-start | bytes 454664 | tf_op jit(solution)/shard_map/ppermute | solution.py:601
  4.2 4.1 %collective-permute-start.1 = (f32[37,8,128]{2,1,0:T(8,128)S(1)}, f32[37,8,128]{2,1,0:T(8,128)S(1)}, u32[]{:S(2)}, u32[]{:S(2)}) collective-permute-start(f32[37,8,128]{2,1,0:T(8,128)S(1)} %get-tuple-element.24.refs_3_), channel_id=1, source_target_pairs={{1,2},{2,1},{3,4},{4,3},{5,6},{6,5},{9,10},{10,9},{11,12},{12,11},... | collective-permute-start | bytes 454664 | tf_op jit(solution)/shard_map/ppermute | solution.py:600
  8.4 10.7 %collective-permute-start.2 = (f32[22,8,128]{2,1,0:T(8,128)S(1)}, f32[22,8,128]{2,1,0:T(8,128)S(1)}, u32[]{:S(2)}, u32[]{:S(2)}) collective-permute-start(f32[22,8,128]{2,1,0:T(8,128)S(1)} %get-tuple-element.34), channel_id=1, source_target_pairs={{0,8},{8,0},{16,24},{24,16},{1,9},{9,1},{17,25},{25,17},{2,10},{10... | collective-permute-start | bytes 270344 | tf_op jit(solution)/shard_map/ppermute | solution.py:621
  11.0 8.2 %collective-permute-start.3 = (f32[22,8,128]{2,1,0:T(8,128)S(1)}, f32[22,8,128]{2,1,0:T(8,128)S(1)}, u32[]{:S(2)}, u32[]{:S(2)}) collective-permute-start(f32[22,8,128]{2,1,0:T(8,128)S(1)} %get-tuple-element.35), channel_id=1, source_target_pairs={{8,16},{16,8},{9,17},{17,9},{10,18},{18,10},{11,19},{19,11},{12,20... | collective-permute-start | bytes 270344 | tf_op jit(solution)/shard_map/ppermute | solution.py:622
  11.8 2.1 %copy-start = (s32[256,128]{1,0:T(8,128)S(1)}, s32[256,128]{1,0:T(8,128)}, u32[]{:S(2)}) copy-start(s32[256,128]{1,0:T(8,128)} %refs_10_.3) | copy-start | bytes 393220
  11.8 2.0 %copy-start.1 = (f32[256,128]{1,0:T(8,128)S(1)}, f32[256,128]{1,0:T(8,128)}, u32[]{:S(2)}) copy-start(f32[256,128]{1,0:T(8,128)} %refs_11_.1) | copy-start | bytes 393220
  21.7 17.2 %all-to-all-start = ((f32[32,1,128]{2,1,0:T(1,128)}), f32[32,1,128]{2,1,0:T(1,128)S(1)}, u32[]{:S(2)}, u32[]{:S(2)}) async-start(f32[32,1,128]{2,1,0:T(1,128)} %bitcast.5), calls=%async_computation | async-start | bytes 32768 | tf_op jit(solution)/shard_map/all_to_all | solution.py:672

commit v4 on v3

--- a/solution.py
+++ b/solution.py
@@ -43,7 +43,7 @@
     written = {}
     for i in range(-2 * lag, len(items)):
         if i + 2 * lag < len(items):
-            h_in, _, _, _, _, _, r, has_above, below = items[i + 2 * lag]
+            h_in, _, _, _, _, _, r, has_above, below, *beside = items[i + 2 * lag]
             assert written.get((id(h_in), r), -(10**9)) < i
             height = h_in[r]
             live[i + 2 * lag] = [
@@ -52,16 +52,19 @@
                 h_in[r - 1] if has_above else None,
                 h_in[r + 1] if below == "row" else None,
                 None,
-                None,
+                roll(height, 1) if beside else None,
             ]
         if 0 <= i + lag < len(items):
             state = live[i + lag]
             coef_y, r = items[i + lag][5], items[i + lag][6]
             along = coef_y[pl.ds(r, 1), :] * (state[1] - state[0])
             state[4] = along
-            state[5] = roll(along, 1)
+            if len(items[i + lag]) > 9:
+                state[5] = items[i + lag][9][pl.ds(r, 1), :] * (state[0] - state[5])
+            else:
+                state[5] = roll(along, 1)
         if i >= 0:
-            h_in, d_in, h_out, d_out, coef_x, _, r, has_above, below = items[i]
+            h_in, d_in, h_out, d_out, coef_x, _, r, has_above, below = items[i][:9]
             height, _, above, under, along, along_before = live.pop(i)
             if below == "item":
                 under = live[i + 1][0]
@@ -386,7 +389,7 @@
 
 def bands_kernel(
     rows, x_even_in, x_odd_in, h_ref, d_ref, cx_ref, cy_ref, bh0, bd0, cbx, cby, done_wet, uplift_ref, sums_ref, homes_ref,
-    edge, message, hs, ds, cxs, cys,
+    edge, message, hs, ds, cxs, cys, cbs,
 ):
     lane = lanes_of()
     second = second_lanes(lane)
@@ -457,13 +460,17 @@
             store(ds, (band, place), divergence)
     store.release()
 
+    for b in range(3):
+        for low in range(0, depth, W):
+            store(cbs, (b, slice(low, low + W)), roll(cys[b, low : low + W, :], 1))
+    store.release()
     views = [(hs.at[b], ds.at[b], hs.at[b], ds.at[b], cxs.at[b], cys.at[b]) for b in range(3)]
     items = []
     for t in range(1, ITERS + 1):
         low, high = t, depth - t
-        for view in views:
+        for b, view in enumerate(views):
             for r in range(low, high):
-                items.append(view + (r, r == low, "item" if r + 1 < high else "row"))
+                items.append(view + (r, r == low, "item" if r + 1 < high else "row", cbs.at[b]))
     advance(items, 8)
 
     bounds = slot_bounds(rows)
@@ -662,6 +669,7 @@
             pltpu.VMEM((3, depth, 8, columns), F32),
             pltpu.VMEM((3, depth, columns), F32),
             pltpu.VMEM((3, depth, columns), F32),
+            pltpu.VMEM((3, depth, columns), F32),
         ],
         compiler_params=params(2),
         name="bands",
@@ -686,7 +694,7 @@
 
 LOAD_MIB = 6
 COST = 40_000_000
-EARLY = 5
+EARLY = 6
 
 
 def solution(mesh):

time: 39.8 us -> 38.5 us (0.967)
  Pallas kernels: 17.6 us -> 16.9 us
  starting transfers between devices: 14.6 us -> 13.9 us
    pallas_call x1, Pallas kernels: 2.54 us -> 1.83 us  [body(): pl.pallas_call(bind(bands_kernel, rows), out_shape=(shaped(2 * W, gauges,...]
    pallas_call x1, Pallas kernels: 3.39 us -> 4.08 us  [body(): pl.pallas_call(bind(center_first_kernel, rows, range(EARLY)), out_shape=(...]
    pallas_call x1, Pallas kernels: 2.02 us -> 1.39 us  [body(): pl.pallas_call(bind(center_second_kernel, rows, range(EARLY, ITERS)), out...]
    all_to_all x1, starting transfers between devices: 10 us -> 9.4 us  [body(): received = lax.all_to_all(message, ('gx', 'gy'), 0, 0, tiled=True)]
  transfers between devices with their start and end apart: 5 -> 5, of which waited for: 1 -> 1; matrix products, arithmetic and copies ran while one was open for 0% -> 0% of each run, Pallas kernels for 30% -> 31%
where the time goes in v4:
time: 38.5 us; the launch traced here: 38.3 us
  Pallas kernels  16.9 us (44%)
  starting transfers between devices  13.9 us (36%)
  waiting for transfers between devices  5.94 us (15%)
  between operations  0.75 us (2%)
  local copies, waits for them, and re-layouts  0.69 us (2%)
    all_to_all x1, starting transfers between devices, body(): received = lax.all_to_all(message, ('gx', 'gy'), 0, 0, tiled=True)  9.4 us
    all_to_all x1, waiting for transfers between devices, body(): received = lax.all_to_all(message, ('gx', 'gy'), 0, 0, tiled=True)  5.93 us
    pallas_call x1, Pallas kernels, body(): pl.pallas_call(bind(strips_kernel, rows), out_shape=(shaped(rows, gauges,...  5.23 us
    pallas_call x1, Pallas kernels, body(): pl.pallas_call(bind(center_first_kernel, rows, range(EARLY)), out_shape=(...  4.08 us
    pallas_call x1, Pallas kernels, body(): pl.pallas_call(bind(load_kernel, rows), out_shape=(shaped(*layers), shape...  3.04 us
    ppermute x1, starting transfers between devices, body(): x_even_in = lax.ppermute(x_even_out, 'gx', pairs('gx', 0))  2.52 us
    pallas_call x1, Pallas kernels, body(): pl.pallas_call(bind(bands_kernel, rows), out_shape=(shaped(2 * W, gauges,...  1.83 us
    pallas_call x1, Pallas kernels, body(): pl.pallas_call(bind(center_second_kernel, rows, range(EARLY, ITERS)), out...  1.39 us
  transfers between devices with their start and end apart: 5, of which 1 were waited for; matrix products, arithmetic and copies ran while one was open for 0% of the time, Pallas kernels for 31%

profile of v4, /device:TPU:0, one launch (start us, length us, event | category | flops | bytes accessed | tf_op | source)
XLA Modules:
  0.0 38.3 jit_solution(7044294349963608170)
XLA Ops:
  0.6 3.0 %load.1 = (f32[264,8,128]{2,1,0:T(8,128)S(1)}, f32[264,8,128]{2,1,0:T(8,128)S(1)}, f32[37,8,128]{2,1,0:T(8,128)S(1)}, f32[37,8,128]{2,1,0:T(8,128)S(1)}, f32[256...) custom-call(f32[2048,128]{1,0:T(8,128)} %bitcast.9, f32[2048,128]{1,0:T(8,128)} %bitcast.10, ...), custom_call_target="tpu_custom_call" | custom-call | tf_op jit(solution)/shard_map/load/pallas_call | solution.py:580
  3.7 0.5 %collective-permute-start = (f32[37,8,128]{2,1,0:T(8,128)S(1)}, f32[37,8,128]{2,1,0:T(8,128)S(1)}, u32[]{:S(2)}, u32[]{:S(2)}) collective-permute-start(f32[37,8,128]{2,1,0:T(8,128)S(1)} %get-tuple-element.23.refs_2_), channel_id=1, source_target_pairs={{0,1},{1,0},{2,3},{3,2},{4,5},{5,4},{6,7},{7,6},{8,9},{9,8},{10,11... | collective-permute-start | bytes 454664 | tf_op jit(solution)/shard_map/ppermute | solution.py:608
  4.2 0.7 %collective-permute-start.1 = (f32[37,8,128]{2,1,0:T(8,128)S(1)}, f32[37,8,128]{2,1,0:T(8,128)S(1)}, u32[]{:S(2)}, u32[]{:S(2)}) collective-permute-start(f32[37,8,128]{2,1,0:T(8,128)S(1)} %get-tuple-element.24.refs_3_), channel_id=1, source_target_pairs={{1,2},{2,1},{3,4},{4,3},{5,6},{6,5},{9,10},{10,9},{11,12},{12,11},... | collective-permute-start | bytes 454664 | tf_op jit(solution)/shard_map/ppermute | solution.py:607
  4.9 4.1 %center_first.1 = (f32[264,8,128]{2,1,0:T(8,128)S(1)}, f32[264,8,128]{2,1,0:T(8,128)S(1)}, f32[8,128]{1,0:T(8,128)S(1)}) custom-call(f32[264,8,128]{2,1,0:T(8,128)S(1)} %get-tuple-element.25.refs_0_.refs_4_.refs_2_, f32[264,8,128]{2,1,0:T(8,128)S(1)} %get-tuple-element.26.refs_1_.refs_5_.refs_3_, f32[256,128]{1,0:T(8,128)S(1)} %get-tuple-element.27.refs_2_.refs_6_.refs_4_, ...), custom_call_target="tpu_custom_call" | custom-call | flops 40000000 | bytes 1048576 | tf_op jit(solution)/shard_map/center_first/pallas_call | solution.py:610
  8.9 0.0 collective-permute-done.refs_0_
  9.0 0.0 collective-permute-done.1.refs_1_
  9.0 0.2 middle.1
  9.1 2.5 %collective-permute-start.2 = (f32[22,8,128]{2,1,0:T(8,128)S(1)}, f32[22,8,128]{2,1,0:T(8,128)S(1)}, u32[]{:S(2)}, u32[]{:S(2)}) collective-permute-start(f32[22,8,128]{2,1,0:T(8,128)S(1)} %get-tuple-element.34), channel_id=1, source_target_pairs={{0,8},{8,0},{16,24},{24,16},{1,9},{9,1},{17,25},{25,17},{2,10},{10... | collective-permute-start | bytes 270344 | tf_op jit(solution)/shard_map/ppermute | solution.py:628
  11.6 0.8 %collective-permute-start.3 = (f32[22,8,128]{2,1,0:T(8,128)S(1)}, f32[22,8,128]{2,1,0:T(8,128)S(1)}, u32[]{:S(2)}, u32[]{:S(2)}) collective-permute-start(f32[22,8,128]{2,1,0:T(8,128)S(1)} %get-tuple-element.35), channel_id=1, source_target_pairs={{8,16},{16,8},{9,17},{17,9},{10,18},{18,10},{11,19},{19,11},{12,20... | collective-permute-start | bytes 270344 | tf_op jit(solution)/shard_map/ppermute | solution.py:629
  12.5 0.0 copy-start
  12.5 0.0 copy-start.1
  12.5 1.4 %center_second.1 = (f32[264,8,128]{2,1,0:T(8,128)S(1)}, f32[264,8,128]{2,1,0:T(8,128)S(1)}) custom-call(f32[264,8,128]{2,1,0:T(8,128)S(1)} %get-tuple-element.29.refs_0_, f32[264,8,128]{2,1,0:T(8,128)S(1)} %get-tuple-element.30.refs_1_, f32[256,128]{1,0:T(8,128)S(1)} %get-tuple-element.27.refs_2_.refs_6_.refs_4_, ...), custom_call_target="tpu_custom_call", output_to_operand_aliasing={{0}: (0, {}), {1}: (1, {})} | custom-call | flops 40000000 | bytes 1048576 | tf_op jit(solution)/shard_map/center_second/pallas_call | solution.py:631
  13.9 0.0 copy-done
  13.9 0.0 copy-done.1
  13.9 5.2 %strips.1 = (f32[256,8,128]{2,1,0:T(8,128)S(1)}, f32[144,8,128]{2,1,0:T(8,128)S(1)}, f32[144,8,128]{2,1,0:T(8,128)S(1)}, f32[136,128]{1,0:T(8,128)S(1)}, f32[136...) custom-call(f32[37,8,128]{2,1,0:T(8,128)S(1)} %collective-permute-done.refs_0_, ...), custom_call_target="tpu_custom_call" | custom-call | flops 40000000 | bytes 1048576 | tf_op jit(solution)/shard_map/strips/pallas_call | solution.py:644
  19.2 0.0 collective-permute-done.2.refs_0_
  19.2 0.0 collective-permute-done.3.refs_1_
  19.2 1.8 %bands.1 = (f32[16,8,128]{2,1,0:T(8,128)S(1)}, f32[32,128]{1,0:T(8,128)}) custom-call(f32[22,8,128]{2,1,0:T(8,128)S(1)} %collective-permute-done.2.refs_0_, f32[22,8,128]{2,1,0:T(8,128)S(1)} %collective-permute-done.3.refs_1_, f32[264,8,128]{2,1,0:T(8,128)S(1)} %get-tuple-element.25.refs_0_.refs_4_.refs_2_, ...), custom_call_target="tpu_custom_call" | custom-call | tf_op jit(solution)/shard_map/bands/pallas_call | solution.py:662
  21.0 9.4 %all-to-all-start = ((f32[32,1,128]{2,1,0:T(1,128)}), f32[32,1,128]{2,1,0:T(1,128)S(1)}, u32[]{:S(2)}, u32[]{:S(2)}) async-start(f32[32,1,128]{2,1,0:T(1,128)} %bitcast.5), calls=%async_computation | async-start | bytes 32768 | tf_op jit(solution)/shard_map/all_to_all | solution.py:680
  30.4 1.2 %write.1 = f32[2048,128]{1,0:T(8,128)} custom-call(f32[256,8,128]{2,1,0:T(8,128)S(1)} %get-tuple-element.32.refs_0_, f32[16,8,128]{2,1,0:T(8,128)S(1)} %get-tuple-element.42.refs_1_), custom_call_target="tpu_custom_call" | custom-call | tf_op jit(solution)/shard_map/write/pallas_call | solution.py:681
  31.6 5.9 %all-to-all-done = f32[32,1,128]{2,1,0:T(1,128)S(1)} async-done(((f32[32,1,128]{2,1,0:T(1,128)}), f32[32,1,128]{2,1,0:T(1,128)S(1)}, u32[]{:S(2)}, u32[]{:S(2)}) %all-to-all-start) | async-done | bytes 16416 | tf_op jit(solution)/shard_map/all_to_all | solution.py:680
  37.6 0.1 reduce_sum.9
  37.6 0.7 %reshape.33 = f32[8,8]{1,0:T(8,128)} reshape(f32[64]{0:T(128)S(1)} %bitcast.12) | data formatting | bytes 512 | tf_op jit(solution)/shard_map/reshape | solution.py:691
Async XLA Ops:
  3.7 5.3 %collective-permute-start = (f32[37,8,128]{2,1,0:T(8,128)S(1)}, f32[37,8,128]{2,1,0:T(8,128)S(1)}, u32[]{:S(2)}, u32[]{:S(2)}) collective-permute-start(f32[37,8,128]{2,1,0:T(8,128)S(1)} %get-tuple-element.23.refs_2_), channel_id=1, source_target_pairs={{0,1},{1,0},{2,3},{3,2},{4,5},{5,4},{6,7},{7,6},{8,9},{9,8},{10,11... | collective-permute-start | bytes 454664 | tf_op jit(solution)/shard_map/ppermute | solution.py:608
  4.2 4.8 %collective-permute-start.1 = (f32[37,8,128]{2,1,0:T(8,128)S(1)}, f32[37,8,128]{2,1,0:T(8,128)S(1)}, u32[]{:S(2)}, u32[]{:S(2)}) collective-permute-start(f32[37,8,128]{2,1,0:T(8,128)S(1)} %get-tuple-element.24.refs_3_), channel_id=1, source_target_pairs={{1,2},{2,1},{3,4},{4,3},{5,6},{6,5},{9,10},{10,9},{11,12},{12,11},... | collective-permute-start | bytes 454664 | tf_op jit(solution)/shard_map/ppermute | solution.py:607
  9.1 10.0 %collective-permute-start.2 = (f32[22,8,128]{2,1,0:T(8,128)S(1)}, f32[22,8,128]{2,1,0:T(8,128)S(1)}, u32[]{:S(2)}, u32[]{:S(2)}) collective-permute-start(f32[22,8,128]{2,1,0:T(8,128)S(1)} %get-tuple-element.34), channel_id=1, source_target_pairs={{0,8},{8,0},{16,24},{24,16},{1,9},{9,1},{17,25},{25,17},{2,10},{10... | collective-permute-start | bytes 270344 | tf_op jit(solution)/shard_map/ppermute | solution.py:628
  11.6 7.5 %collective-permute-start.3 = (f32[22,8,128]{2,1,0:T(8,128)S(1)}, f32[22,8,128]{2,1,0:T(8,128)S(1)}, u32[]{:S(2)}, u32[]{:S(2)}) collective-permute-start(f32[22,8,128]{2,1,0:T(8,128)S(1)} %get-tuple-element.35), channel_id=1, source_target_pairs={{8,16},{16,8},{9,17},{17,9},{10,18},{18,10},{11,19},{19,11},{12,20... | collective-permute-start | bytes 270344 | tf_op jit(solution)/shard_map/ppermute | solution.py:629
  12.5 1.4 %copy-start = (s32[256,128]{1,0:T(8,128)S(1)}, s32[256,128]{1,0:T(8,128)}, u32[]{:S(2)}) copy-start(s32[256,128]{1,0:T(8,128)} %refs_10_.3) | copy-start | bytes 393220
  12.5 1.4 %copy-start.1 = (f32[256,128]{1,0:T(8,128)S(1)}, f32[256,128]{1,0:T(8,128)}, u32[]{:S(2)}) copy-start(f32[256,128]{1,0:T(8,128)} %refs_11_.1) | copy-start | bytes 393220
  21.0 16.5 %all-to-all-start = ((f32[32,1,128]{2,1,0:T(1,128)}), f32[32,1,128]{2,1,0:T(1,128)S(1)}, u32[]{:S(2)}, u32[]{:S(2)}) async-start(f32[32,1,128]{2,1,0:T(1,128)} %bitcast.5), calls=%async_computation | async-start | bytes 32768 | tf_op jit(solution)/shard_map/all_to_all | solution.py:680

commit v5 on v4

--- a/solution.py
+++ b/solution.py
@@ -110,25 +110,25 @@
     h_out, d_out, odd_out, even_out, cx_ref, cy_ref, homes, hb, xb, yb, wet_ref, lists_ref, home_ref, sems,
 ):
     gauges = 8
-    parts = 4
+    parts, fields = 2, 3
     size = rows // parts
     plain = [
-        pltpu.make_async_copy(source, target, sems.at[parts + i])
+        pltpu.make_async_copy(source, target, sems.at[parts * fields + i])
         for i, (source, target) in enumerate(((cx_hbm, cx_ref), (cy_hbm, cy_ref), (wet_hbm, wet_ref)))
     ]
     scalars = [
-        pltpu.make_async_copy(lists_hbm, lists_ref, sems.at[parts + 3]),
-        pltpu.make_async_copy(home_hbm, home_ref, sems.at[parts + 4]),
+        pltpu.make_async_copy(lists_hbm, lists_ref, sems.at[parts * fields + 3]),
+        pltpu.make_async_copy(home_hbm, home_ref, sems.at[parts * fields + 4]),
     ]
     for copy in plain + scalars:
         copy.start()
     for part in range(parts):
-        for source, target in ((y_hbm, yb), (x_hbm, xb), (h_hbm, hb)):
+        for field, (source, target) in enumerate(((y_hbm, yb), (x_hbm, xb), (h_hbm, hb))):
             for gauge in range(gauges):
                 pltpu.make_async_copy(
                     source.at[pl.ds(gauge * rows + part * size, size)],
                     target.at[pl.ds(part * size, size), gauge],
-                    sems.at[part],
+                    sems.at[part * fields + field],
                 ).start()
 
     even = lax.rem(lax.axis_index("gy"), 2) == 0
@@ -183,8 +183,9 @@
     above, sides = None, None
     lag = 16
     for part in range(parts):
-        done = hb.at[pl.ds(0, 3 * size)]
-        pltpu.make_async_copy(done, done, sems.at[part]).wait()
+        for field, target in enumerate((yb, xb, hb)):
+            done = target.at[pl.ds(part * size, size)]
+            pltpu.make_async_copy(done, done, sems.at[part * fields + field]).wait()
         low, high = part * size, (part + 1) * size
         for r in range(low - lag, high):
             if r + lag < high:
@@ -590,7 +591,7 @@
             pltpu.VMEM((rows, columns), jnp.int32),
             pltpu.SMEM(tile_patches.shape, jnp.int32),
             pltpu.SMEM(patch_home.shape, jnp.int32),
-            pltpu.SemaphoreType.DMA((9,)),
+            pltpu.SemaphoreType.DMA((11,)),
         ],
         compiler_params=params(LOAD_MIB),
         name="load",

time: 38.5 us -> 38.6 us (level)
  no operation moved by 1% of the time
where the time goes in v5:
time: 38.6 us; the launch traced here: 38.4 us
  Pallas kernels  17 us (44%)
  starting transfers between devices  13.9 us (36%)
  waiting for transfers between devices  5.94 us (15%)
  between operations  0.75 us (2%)
  local copies, waits for them, and re-layouts  0.69 us (2%)
    all_to_all x1, starting transfers between devices, body(): received = lax.all_to_all(message, ('gx', 'gy'), 0, 0, tiled=True)  9.4 us
    all_to_all x1, waiting for transfers between devices, body(): received = lax.all_to_all(message, ('gx', 'gy'), 0, 0, tiled=True)  5.93 us
    pallas_call x1, Pallas kernels, body(): pl.pallas_call(bind(strips_kernel, rows), out_shape=(shaped(rows, gauges,...  5.23 us
    pallas_call x1, Pallas kernels, body(): pl.pallas_call(bind(center_first_kernel, rows, range(EARLY)), out_shape=(...  4.08 us
    pallas_call x1, Pallas kernels, body(): pl.pallas_call(bind(load_kernel, rows), out_shape=(shaped(*layers), shape...  3.16 us
    ppermute x1, starting transfers between devices, body(): x_even_in = lax.ppermute(x_even_out, 'gx', pairs('gx', 0))  2.52 us
    pallas_call x1, Pallas kernels, body(): pl.pallas_call(bind(bands_kernel, rows), out_shape=(shaped(2 * W, gauges,...  1.83 us
    pallas_call x1, Pallas kernels, body(): pl.pallas_call(bind(center_second_kernel, rows, range(EARLY, ITERS)), out...  1.39 us
  transfers between devices with their start and end apart: 5, of which 1 were waited for; matrix products, arithmetic and copies ran while one was open for 0% of the time, Pallas kernels for 31%

profile of v5, /device:TPU:0, one launch (start us, length us, event | category | flops | bytes accessed | tf_op | source)
XLA Modules:
  0.0 38.4 jit_solution(16607427060014254158)
XLA Ops:
  0.6 3.2 %load.1 = (f32[264,8,128]{2,1,0:T(8,128)S(1)}, f32[264,8,128]{2,1,0:T(8,128)S(1)}, f32[37,8,128]{2,1,0:T(8,128)S(1)}, f32[37,8,128]{2,1,0:T(8,128)S(1)}, f32[256...) custom-call(f32[2048,128]{1,0:T(8,128)} %bitcast.9, f32[2048,128]{1,0:T(8,128)} %bitcast.10, ...), custom_call_target="tpu_custom_call" | custom-call | tf_op jit(solution)/shard_map/load/pallas_call | solution.py:581
  3.8 0.5 %collective-permute-start = (f32[37,8,128]{2,1,0:T(8,128)S(1)}, f32[37,8,128]{2,1,0:T(8,128)S(1)}, u32[]{:S(2)}, u32[]{:S(2)}) collective-permute-start(f32[37,8,128]{2,1,0:T(8,128)S(1)} %get-tuple-element.23.refs_2_), channel_id=1, source_target_pairs={{0,1},{1,0},{2,3},{3,2},{4,5},{5,4},{6,7},{7,6},{8,9},{9,8},{10,11... | collective-permute-start | bytes 454664 | tf_op jit(solution)/shard_map/ppermute | solution.py:609
  4.3 0.7 %collective-permute-start.1 = (f32[37,8,128]{2,1,0:T(8,128)S(1)}, f32[37,8,128]{2,1,0:T(8,128)S(1)}, u32[]{:S(2)}, u32[]{:S(2)}) collective-permute-start(f32[37,8,128]{2,1,0:T(8,128)S(1)} %get-tuple-element.24.refs_3_), channel_id=1, source_target_pairs={{1,2},{2,1},{3,4},{4,3},{5,6},{6,5},{9,10},{10,9},{11,12},{12,11},... | collective-permute-start | bytes 454664 | tf_op jit(solution)/shard_map/ppermute | solution.py:608
  5.0 4.1 %center_first.1 = (f32[264,8,128]{2,1,0:T(8,128)S(1)}, f32[264,8,128]{2,1,0:T(8,128)S(1)}, f32[8,128]{1,0:T(8,128)S(1)}) custom-call(f32[264,8,128]{2,1,0:T(8,128)S(1)} %get-tuple-element.25.refs_0_.refs_4_.refs_2_, f32[264,8,128]{2,1,0:T(8,128)S(1)} %get-tuple-element.26.refs_1_.refs_5_.refs_3_, f32[256,128]{1,0:T(8,128)S(1)} %get-tuple-element.27.refs_2_.refs_6_.refs_4_, ...), custom_call_target="tpu_custom_call" | custom-call | flops 40000000 | bytes 1048576 | tf_op jit(solution)/shard_map/center_first/pallas_call | solution.py:611
  9.1 0.0 collective-permute-done.refs_0_
  9.1 0.0 collective-permute-done.1.refs_1_
  9.1 0.2 middle.1
  9.2 2.5 %collective-permute-start.2 = (f32[22,8,128]{2,1,0:T(8,128)S(1)}, f32[22,8,128]{2,1,0:T(8,128)S(1)}, u32[]{:S(2)}, u32[]{:S(2)}) collective-permute-start(f32[22,8,128]{2,1,0:T(8,128)S(1)} %get-tuple-element.34), channel_id=1, source_target_pairs={{0,8},{8,0},{16,24},{24,16},{1,9},{9,1},{17,25},{25,17},{2,10},{10... | collective-permute-start | bytes 270344 | tf_op jit(solution)/shard_map/ppermute | solution.py:629
  11.8 0.8 %collective-permute-start.3 = (f32[22,8,128]{2,1,0:T(8,128)S(1)}, f32[22,8,128]{2,1,0:T(8,128)S(1)}, u32[]{:S(2)}, u32[]{:S(2)}) collective-permute-start(f32[22,8,128]{2,1,0:T(8,128)S(1)} %get-tuple-element.35), channel_id=1, source_target_pairs={{8,16},{16,8},{9,17},{17,9},{10,18},{18,10},{11,19},{19,11},{12,20... | collective-permute-start | bytes 270344 | tf_op jit(solution)/shard_map/ppermute | solution.py:630
  12.6 0.0 copy-start
  12.6 0.0 copy-start.1
  12.6 1.4 %center_second.1 = (f32[264,8,128]{2,1,0:T(8,128)S(1)}, f32[264,8,128]{2,1,0:T(8,128)S(1)}) custom-call(f32[264,8,128]{2,1,0:T(8,128)S(1)} %get-tuple-element.29.refs_0_, f32[264,8,128]{2,1,0:T(8,128)S(1)} %get-tuple-element.30.refs_1_, f32[256,128]{1,0:T(8,128)S(1)} %get-tuple-element.27.refs_2_.refs_6_.refs_4_, ...), custom_call_target="tpu_custom_call", output_to_operand_aliasing={{0}: (0, {}), {1}: (1, {})} | custom-call | flops 40000000 | bytes 1048576 | tf_op jit(solution)/shard_map/center_second/pallas_call | solution.py:632
  14.0 0.0 copy-done
  14.0 0.0 copy-done.1
  14.0 5.2 %strips.1 = (f32[256,8,128]{2,1,0:T(8,128)S(1)}, f32[144,8,128]{2,1,0:T(8,128)S(1)}, f32[144,8,128]{2,1,0:T(8,128)S(1)}, f32[136,128]{1,0:T(8,128)S(1)}, f32[136...) custom-call(f32[37,8,128]{2,1,0:T(8,128)S(1)} %collective-permute-done.refs_0_, ...), custom_call_target="tpu_custom_call" | custom-call | flops 40000000 | bytes 1048576 | tf_op jit(solution)/shard_map/strips/pallas_call | solution.py:645
  19.3 0.0 collective-permute-done.2.refs_0_
  19.3 0.0 collective-permute-done.3.refs_1_
  19.3 1.8 %bands.1 = (f32[16,8,128]{2,1,0:T(8,128)S(1)}, f32[32,128]{1,0:T(8,128)}) custom-call(f32[22,8,128]{2,1,0:T(8,128)S(1)} %collective-permute-done.2.refs_0_, f32[22,8,128]{2,1,0:T(8,128)S(1)} %collective-permute-done.3.refs_1_, f32[264,8,128]{2,1,0:T(8,128)S(1)} %get-tuple-element.25.refs_0_.refs_4_.refs_2_, ...), custom_call_target="tpu_custom_call" | custom-call | tf_op jit(solution)/shard_map/bands/pallas_call | solution.py:663
  21.1 9.4 %all-to-all-start = ((f32[32,1,128]{2,1,0:T(1,128)}), f32[32,1,128]{2,1,0:T(1,128)S(1)}, u32[]{:S(2)}, u32[]{:S(2)}) async-start(f32[32,1,128]{2,1,0:T(1,128)} %bitcast.5), calls=%async_computation | async-start | bytes 32768 | tf_op jit(solution)/shard_map/all_to_all | solution.py:681
  30.6 1.2 %write.1 = f32[2048,128]{1,0:T(8,128)} custom-call(f32[256,8,128]{2,1,0:T(8,128)S(1)} %get-tuple-element.32.refs_0_, f32[16,8,128]{2,1,0:T(8,128)S(1)} %get-tuple-element.42.refs_1_), custom_call_target="tpu_custom_call" | custom-call | tf_op jit(solution)/shard_map/write/pallas_call | solution.py:682
  31.8 5.9 %all-to-all-done = f32[32,1,128]{2,1,0:T(1,128)S(1)} async-done(((f32[32,1,128]{2,1,0:T(1,128)}), f32[32,1,128]{2,1,0:T(1,128)S(1)}, u32[]{:S(2)}, u32[]{:S(2)}) %all-to-all-start) | async-done | bytes 16416 | tf_op jit(solution)/shard_map/all_to_all | solution.py:681
  37.7 0.1 reduce_sum.9
  37.7 0.7 %reshape.33 = f32[8,8]{1,0:T(8,128)} reshape(f32[64]{0:T(128)S(1)} %bitcast.12) | data formatting | bytes 512 | tf_op jit(solution)/shard_map/reshape | solution.py:692
Async XLA Ops:
  3.8 5.3 %collective-permute-start = (f32[37,8,128]{2,1,0:T(8,128)S(1)}, f32[37,8,128]{2,1,0:T(8,128)S(1)}, u32[]{:S(2)}, u32[]{:S(2)}) collective-permute-start(f32[37,8,128]{2,1,0:T(8,128)S(1)} %get-tuple-element.23.refs_2_), channel_id=1, source_target_pairs={{0,1},{1,0},{2,3},{3,2},{4,5},{5,4},{6,7},{7,6},{8,9},{9,8},{10,11... | collective-permute-start | bytes 454664 | tf_op jit(solution)/shard_map/ppermute | solution.py:609
  4.3 4.8 %collective-permute-start.1 = (f32[37,8,128]{2,1,0:T(8,128)S(1)}, f32[37,8,128]{2,1,0:T(8,128)S(1)}, u32[]{:S(2)}, u32[]{:S(2)}) collective-permute-start(f32[37,8,128]{2,1,0:T(8,128)S(1)} %get-tuple-element.24.refs_3_), channel_id=1, source_target_pairs={{1,2},{2,1},{3,4},{4,3},{5,6},{6,5},{9,10},{10,9},{11,12},{12,11},... | collective-permute-start | bytes 454664 | tf_op jit(solution)/shard_map/ppermute | solution.py:608
  9.2 10.0 %collective-permute-start.2 = (f32[22,8,128]{2,1,0:T(8,128)S(1)}, f32[22,8,128]{2,1,0:T(8,128)S(1)}, u32[]{:S(2)}, u32[]{:S(2)}) collective-permute-start(f32[22,8,128]{2,1,0:T(8,128)S(1)} %get-tuple-element.34), channel_id=1, source_target_pairs={{0,8},{8,0},{16,24},{24,16},{1,9},{9,1},{17,25},{25,17},{2,10},{10... | collective-permute-start | bytes 270344 | tf_op jit(solution)/shard_map/ppermute | solution.py:629
  11.8 7.5 %collective-permute-start.3 = (f32[22,8,128]{2,1,0:T(8,128)S(1)}, f32[22,8,128]{2,1,0:T(8,128)S(1)}, u32[]{:S(2)}, u32[]{:S(2)}) collective-permute-start(f32[22,8,128]{2,1,0:T(8,128)S(1)} %get-tuple-element.35), channel_id=1, source_target_pairs={{8,16},{16,8},{9,17},{17,9},{10,18},{18,10},{11,19},{19,11},{12,20... | collective-permute-start | bytes 270344 | tf_op jit(solution)/shard_map/ppermute | solution.py:630
  12.6 1.4 %copy-start = (s32[256,128]{1,0:T(8,128)S(1)}, s32[256,128]{1,0:T(8,128)}, u32[]{:S(2)}) copy-start(s32[256,128]{1,0:T(8,128)} %refs_10_.3) | copy-start | bytes 393220
  12.6 1.4 %copy-start.1 = (f32[256,128]{1,0:T(8,128)S(1)}, f32[256,128]{1,0:T(8,128)}, u32[]{:S(2)}) copy-start(f32[256,128]{1,0:T(8,128)} %refs_11_.1) | copy-start | bytes 393220
  21.1 16.5 %all-to-all-start = ((f32[32,1,128]{2,1,0:T(1,128)}), f32[32,1,128]{2,1,0:T(1,128)S(1)}, u32[]{:S(2)}, u32[]{:S(2)}) async-start(f32[32,1,128]{2,1,0:T(1,128)} %bitcast.5), calls=%async_computation | async-start | bytes 32768 | tf_op jit(solution)/shard_map/all_to_all | solution.py:681
